TPU v7x, 32 devices: a whole 2x2x4 slice. The times are simulated.
32 devices in a mesh: gx: 2 (over x), gy: 4 (over z), gz: 4 (over y, core).
Axes of the slice: x: 2, y: 2, z: 4, core: 2. Of those that a mesh axis runs over, the one named last changes fastest.
Arguments:
- pressure: float32 [2, 32, 32, 512], P(None, 'gx', 'gy', 'gz'), may hold values from -6 to 6
- saturation: float32 [3, 2, 32, 32, 512], P(None, None, 'gx', 'gy', 'gz'), may hold values from 0.15 to 0.45
- permeability: float32 [32, 32, 512], P('gx', 'gy', 'gz'), may hold values from 0.5 to 2
- porosity: float32 [32, 32, 512], P('gx', 'gy', 'gz'), may hold values from 0.1 to 0.35
- upwind_flags: int32 [32, 32, 512], P('gx', 'gy', 'gz'), may hold values from 0 to 63
- diag_inverse: float32 [2, 3, 3, 32, 32, 512], P(None, None, None, 'gx', 'gy', 'gz'), may hold values from -0.12 to 0.8, as said below
- seismic_obs: float32 [32, 32, 512], P('gx', 'gy', 'gz'), may hold values from -6 to 6
- well_x: int32 [2, 4, 64], P('gx', 'gy'), may hold values from 0 to 15
- well_y: int32 [2, 4, 64], P('gx', 'gy'), may hold values from 0 to 7
- well_top: int32 [2, 4, 64], P('gx', 'gy'), may hold values from 0 to 255
- well_len: int32 [2, 4, 64], P('gx', 'gy'), may hold values from 128 to 256
- well_bhp: float32 [2, 2, 4, 64], P(None, 'gx', 'gy'), may hold values from -3 to 3
- well_obs: float32 [2, 2, 4, 64], P(None, 'gx', 'gy'), may hold values from -48 to 48
- fault_cell: int32 [32, 16, 128], P(('gx', 'gy', 'gz')), may hold values from 0 to 16383
- fault_count: int32 [32, 16], P(('gx', 'gy', 'gz')), may hold values from 0 to 128, as said below
- fault_trans: float32 [32, 16, 128], P(('gx', 'gy', 'gz')), may hold values from 0.5 to 2, as said below
- fault_up: int32 [32, 16, 128], P(('gx', 'gy', 'gz')), may hold values from 0 to 3, as said below
- region_map: int32 [8, 8, 128], P('gx', 'gy', 'gz'), may hold values from 0 to 1023
Outputs:
- adjoint: float32 [2, 3, 32, 32, 512], P(None, None, 'gx', 'gy', 'gz')
- region_grad: float32 [2, 1024], P(None, ('gx', 'gy', 'gz'))
Inputs may be any that keep to these rules, and one draw needn't show every extreme that they name: fault_count[dev][p] equals fault_count[i * 16 + p][a] of the connection's other end; a device has no connections with itself; in every draw one device of each group of 16 has exactly 128 connections with every other device of its group. `fault_cell`: slot s of dev toward peer p and slot s of that peer toward dev are the two ends of one connection. `fault_trans`: both ends of a connection hold the same transmissibility. `fault_up`: the two ends of a connection hold opposite bits. `diag_inverse`: entries [t][0][0] lie in 0.25 to 0.5, entries [t][u][u] for u = 1, 2 in 0.4 to 0.8, all others in -0.12 to 0.12.
All inputs are finite; a program needn't handle non-finite values.
Results may differ from a plain program's by a relative error of at most 0.0001.
Values sent between devices are 32-bit elements; how exact they have to be, the bound alone decides.
A program may use at most 128 MiB of HBM per device.

v0:
```python
import functools

import jax
import jax.numpy as jnp
from jax import lax
from jax.experimental import pallas as pl
from jax.experimental.pallas import tpu as pltpu
from jax.sharding import PartitionSpec as P

ITERS = 6
BOX = 4
PARAM_REGIONS = 32
MESH = pl.DeviceIdType.MESH
HIGHEST = lax.Precision.HIGHEST

fluid_viscosity = (0.4, 0.5, 1.0)
sigma_sq = 64.0


def phase_mobility(water_sat, oil_sat):
    gas_sat = 1.0 - water_sat - oil_sat
    return [
        water_sat * water_sat / fluid_viscosity[0],
        oil_sat * oil_sat / fluid_viscosity[1],
        gas_sat * gas_sat / fluid_viscosity[2],
    ]


def mobility_slopes(water_sat, oil_sat):
    gas_sat = 1.0 - water_sat - oil_sat
    return (
        2.0 * water_sat / fluid_viscosity[0] - 2.0 * gas_sat / fluid_viscosity[2],
        2.0 * oil_sat / fluid_viscosity[1] - 2.0 * gas_sat / fluid_viscosity[2],
    )


def split_bf16(value):
    high = value.astype(jnp.bfloat16)
    return high, (value - high.astype(jnp.float32)).astype(jnp.bfloat16)


def kernel(
    counts,
    pressure_hbm,
    saturation_hbm,
    perm_hbm,
    porosity_hbm,
    flags_hbm,
    inverse_hbm,
    seismic_hbm,
    well_x_ref,
    well_y_ref,
    well_top_ref,
    well_len_ref,
    bhp_ref,
    obs_ref,
    fault_cell_ref,
    fault_count_ref,
    fault_trans_ref,
    fault_up_ref,
    map_ref,
    lam_ref,
    region_ref,
    pressure_ref,
    saturation_ref,
    perm_ref,
    porosity_ref,
    flags_ref,
    inverse_ref,
    seismic_ref,
    in_sem,
    wp,
    wm,
    src,
    explicit,
    row_hot,
    z_hot,
    fault_coef,
    bx_s,
    by_s,
    bz_s,
    bx_r,
    by_r,
    bz_r,
    b_ss,
    b_rs,
    m_s,
    m_r,
    m_ss,
    m_rs,
    w_s,
    w_r,
    w_ss,
    w_rs,
    x_s,
    y_s,
    z_s,
    x_r,
    y_r,
    z_r,
    f_ss,
    f_rs,
    c_s,
    c_r,
    c_ss,
    c_rs,
    g_s,
    g_r,
    g_ss,
    g_rs,
    r_s,
    r_r,
    r_ss,
    r_rs,
):
    n_gx, n_gy, n_gz = counts
    here = (lax.axis_index("gx"), lax.axis_index("gy"), lax.axis_index("gz"))
    peers = n_gy * n_gz
    me = here[1] * n_gz + here[2]
    shape = perm_ref.shape
    nx, ny, nz = shape
    rows = nx * ny
    slots = m_r.shape[2]
    wide = peers * slots

    def toward(dim, step):
        moved = list(here)
        moved[dim] = lax.rem(here[dim] + step + counts[dim], counts[dim])
        return tuple(moved)

    def peer(offset):
        other = lax.rem(me + offset, peers)
        return (here[0], other // n_gz, lax.rem(other, n_gz))

    def remote(source, target, send, recv, device):
        return pltpu.make_async_remote_copy(
            src_ref=source,
            dst_ref=target,
            send_sem=send,
            recv_sem=recv,
            device_id=device,
            device_id_type=MESH,
        )

    loads = [
        pltpu.make_async_copy(source, target, in_sem.at[n])
        for n, (source, target) in enumerate(
            (
                (perm_hbm, perm_ref),
                (saturation_hbm, saturation_ref),
                (flags_hbm, flags_ref),
                (pressure_hbm, pressure_ref),
                (seismic_hbm, seismic_ref),
                (inverse_hbm, inverse_ref),
                (porosity_hbm, porosity_ref),
            )
        )
    ]
    for load in loads:
        load.start()
    m_r[...] = jnp.zeros_like(m_r)
    c_r[...] = jnp.zeros_like(c_r)

    barrier = pltpu.get_barrier_semaphore()
    for offset in range(1, peers):
        pl.semaphore_signal(barrier, inc=1, device_id=peer(offset), device_id_type=MESH)
    for step in range(1, n_gx):
        pl.semaphore_signal(barrier, inc=1, device_id=toward(0, step), device_id_type=MESH)
    pl.semaphore_wait(barrier, peers - 1 + n_gx - 1)
    for load in loads[:4]:
        load.wait()

    xi = lax.broadcasted_iota(jnp.int32, shape, 0)
    yi = lax.broadcasted_iota(jnp.int32, shape, 1)
    zi = lax.broadcasted_iota(jnp.int32, shape, 2)
    iotas = (xi, yi, zi)
    diagonal = xi == zi

    def pack(column):
        return jnp.sum(jnp.where(diagonal, column, 0.0), axis=0)

    def unpack(tile):
        return jnp.sum(jnp.where(diagonal, tile[None], 0.0), axis=2, keepdims=True)

    def ahead(field, dim, halo):
        if dim == 0:
            return jnp.concatenate([field[1:], halo[None]], axis=0)
        last = shape[dim] - 1
        edge = halo if dim == 1 else unpack(halo)
        return jnp.where(iotas[dim] == last, edge, pltpu.roll(field, last, dim))

    def behind(field, dim, halo):
        if dim == 0:
            return jnp.concatenate([halo[None], field[:-1]], axis=0)
        edge = halo if dim == 1 else unpack(halo)
        return jnp.where(iotas[dim] == 0, edge, pltpu.roll(field, 1, dim))

    perm = perm_ref[...]
    flags = flags_ref[...].astype(jnp.float32)
    pressure = [pressure_ref[t] for t in range(2)]
    mobility = [
        phase_mobility(saturation_ref[t + 1, 0], saturation_ref[t + 1, 1]) for t in range(2)
    ]
    bundle = [perm] + mobility[0] + mobility[1] + [flags] + pressure
    for q, field in enumerate(bundle):
        bx_s[0, q] = field[nx - 1]
        bx_s[1, q] = field[0]
        by_s[0, q] = field[:, ny - 1 :, :]
        by_s[1, q] = field[:, :1, :]
        bz_s[0, q] = pack(field[:, :, nz - 1 :])
        bz_s[1, q] = pack(field[:, :, :1])
    b_copies = []
    for dim, (sent, got) in enumerate(((bx_s, bx_r), (by_s, by_r), (bz_s, bz_r))):
        for side, step in ((0, 1), (1, -1)):
            copy = remote(
                sent.at[side],
                got.at[side],
                b_ss.at[dim, side],
                b_rs.at[dim, side],
                toward(dim, step),
            )
            copy.start()
            b_copies.append(copy)

    def as_row(ref):
        return jnp.concatenate([ref[0, p : p + 1, :] for p in range(peers)], axis=1)

    fault_cell = as_row(fault_cell_ref)
    fault_row = fault_cell // nz
    fault_z = fault_cell - fault_row * nz
    hot = (lax.broadcasted_iota(jnp.int32, (rows, wide), 0) == fault_row).astype(
        jnp.float32
    ).astype(jnp.bfloat16)
    row_hot[:rows] = hot
    row_hot[rows:] = hot
    z_hot[...] = (
        (lax.broadcasted_iota(jnp.int32, (nz, wide), 0) == fault_z)
        .astype(jnp.float32)
        .astype(jnp.bfloat16)
    )

    def gather(fields):
        stacked = []
        for field in fields:
            stacked.append(
                jnp.concatenate(split_bf16(field.reshape(rows, nz).T), axis=1)
            )
        columns = jnp.dot(
            jnp.concatenate(stacked, axis=0), row_hot[...], preferred_element_type=jnp.float32
        )
        chosen = lax.broadcasted_iota(jnp.int32, (nz, wide), 0) == fault_z
        return [
            jnp.sum(
                jnp.where(chosen, columns[k * nz : (k + 1) * nz], 0.0), axis=0, keepdims=True
            )
            for k in range(len(fields))
        ]

    own = gather(mobility[0]) + gather(mobility[1])
    for p in range(peers):
        for q in range(6):
            m_s[p, q : q + 1, :] = own[q][:, p * slots : (p + 1) * slots]
        m_s[p, 6:8, :] = jnp.zeros((2, slots), jnp.float32)
    m_copies = []
    for offset in range(1, peers):
        other = lax.rem(me + offset, peers)
        copy = remote(
            m_s.at[other], m_r.at[me], m_ss.at[offset], m_rs.at[offset], peer(offset)
        )
        copy.start()
        m_copies.append(copy)

    n_wells = well_top_ref.shape[2]
    eye = lax.broadcasted_iota(jnp.int32, (n_wells, n_wells), 0) == lax.broadcasted_iota(
        jnp.int32, (n_wells, n_wells), 1
    )

    def as_column(row):
        return jnp.sum(jnp.where(eye, row.astype(jnp.float32), 0.0), axis=1, keepdims=True)

    well_row = well_x_ref[0] * ny + well_y_ref[0]
    bhp = [as_column(bhp_ref[t, 0]) for t in range(2)]
    well_hot = (
        lax.broadcasted_iota(jnp.int32, (n_wells, rows), 1).astype(jnp.float32)
        == as_column(well_row)
    ).astype(jnp.float32)
    well_hot_t = (
        lax.broadcasted_iota(jnp.int32, (rows, n_wells), 0) == well_row
    ).astype(jnp.float32)
    depth = (here[2] * nz + lax.broadcasted_iota(jnp.int32, (n_wells, nz), 1)).astype(
        jnp.float32
    )
    top = as_column(well_top_ref[0])
    bottom = as_column(well_top_ref[0] + well_len_ref[0])
    perforated = jnp.where((depth >= top) & (depth < bottom), 1.0, 0.0)
    total = [perm * (mobility[t][0] + mobility[t][1] + mobility[t][2]) for t in range(2)]
    lane = lax.broadcasted_iota(jnp.int32, (n_wells, nz), 1)
    rates = jnp.zeros((n_wells, nz), jnp.float32)
    for t in range(2):
        with_pressure = jnp.dot(
            well_hot,
            (total[t] * pressure[t]).reshape(rows, nz),
            precision=HIGHEST,
            preferred_element_type=jnp.float32,
        )
        without = jnp.dot(
            well_hot,
            total[t].reshape(rows, nz),
            precision=HIGHEST,
            preferred_element_type=jnp.float32,
        )
        rate = jnp.sum(
            perforated * (with_pressure - bhp[t] * without), axis=1, keepdims=True
        )
        rates = jnp.where(lane == t, rate, rates)
    w_s[...] = rates
    w_copies = []
    for offset in range(1, n_gz):
        copy = remote(
            w_s, w_r.at[offset], w_ss.at[offset], w_rs.at[offset], toward(2, offset)
        )
        copy.start()
        w_copies.append(copy)

    for copy in b_copies:
        copy.wait()
    halos = ((bx_r, bx_s), (by_r, by_s), (bz_r, bz_s))
    for dim in range(3):
        got = halos[dim][0]
        up_ok = (here[dim] < counts[dim] - 1).astype(jnp.float32)
        low_ok = (here[dim] > 0).astype(jnp.float32)
        up_face = jnp.sqrt(perm * ahead(perm, dim, got[1, 0]))
        up_face = up_face * jnp.where(iotas[dim] == shape[dim] - 1, up_ok, 1.0)
        low_face = jnp.sqrt(perm * behind(perm, dim, got[0, 0]))
        low_face = low_face * jnp.where(iotas[dim] == 0, low_ok, 1.0)
        own_flags = flags.astype(jnp.int32)
        low_flags = behind(flags, dim, got[0, 7]).astype(jnp.int32)
        for t in range(2):
            bit = 3 * t + dim
            own_up = jnp.bitwise_and(jnp.right_shift(own_flags, bit), 1) == 1
            low_up = jnp.bitwise_and(jnp.right_shift(low_flags, bit), 1) == 1
            for k in range(3):
                q = 1 + 3 * t + k
                m = mobility[t][k]
                wp[t, dim, k] = up_face * jnp.where(own_up, m, ahead(m, dim, got[1, q]))
                wm[t, dim, k] = low_face * jnp.where(low_up, behind(m, dim, got[0, q]), m)

    for copy in m_copies:
        copy.wait()
    slot_index = lax.broadcasted_iota(jnp.int32, (1, slots), 1)
    scale = jnp.concatenate(
        [
            jnp.where(
                slot_index < fault_count_ref[:, p : p + 1], fault_trans_ref[0, p : p + 1, :], 0.0
            )
            for p in range(peers)
        ],
        axis=1,
    )
    fault_up = as_row(fault_up_ref)
    for t in range(2):
        own_up = jnp.bitwise_and(jnp.right_shift(fault_up, t), 1) == 1
        for k in range(3):
            q = 3 * t + k
            other = jnp.concatenate([m_r[p, q : q + 1, :] for p in range(peers)], axis=1)
            fault_coef[q : q + 1, :] = scale * jnp.where(own_up, own[q], other)

    for copy in w_copies:
        copy.wait()
    for load in loads[4:]:
        load.wait()
    rates = w_s[...]
    for offset in range(1, n_gz):
        rates = rates + w_r[offset]
    explicit_sum = jnp.zeros(shape, jnp.float32)
    for t in range(2):
        misfit = (rates[:, t : t + 1] - as_column(obs_ref[t, 0])) / sigma_sq
        weight = misfit * perforated
        spread = jnp.dot(
            well_hot_t, weight, precision=HIGHEST, preferred_element_type=jnp.float32
        ).reshape(shape)
        spread_bhp = jnp.dot(
            well_hot_t, weight * bhp[t], precision=HIGHEST, preferred_element_type=jnp.float32
        ).reshape(shape)
        drawn = pressure[t] * spread - spread_bhp
        water_slope, oil_slope = mobility_slopes(
            saturation_ref[t + 1, 0], saturation_ref[t + 1, 1]
        )
        src[t, 0] = total[t] * spread
        water_source = perm * drawn * water_slope
        if t == 1:
            water_source = water_source + saturation_ref[2, 0] - seismic_ref[...]
        src[t, 1] = water_source
        src[t, 2] = perm * drawn * oil_slope
        explicit_sum = explicit_sum + total[t] * drawn
    explicit[...] = explicit_sum

    def relax(t, coupling):
        residual = [src[t, u] for u in range(3)]
        if coupling is not None:
            residual[0] = residual[0] + coupling
        for k in range(3):
            lam_ref[t, k] = (
                inverse_ref[t, 0, k] * residual[0]
                + inverse_ref[t, 1, k] * residual[1]
                + inverse_ref[t, 2, k] * residual[2]
            )

    def face_copies(slot):
        made = []
        for dim, (sent, got) in enumerate(((x_s, x_r), (y_s, y_r), (z_s, z_r))):
            for side, step in ((0, 1), (1, -1)):
                made.append(
                    remote(
                        sent.at[side],
                        got.at[slot, side],
                        f_ss.at[dim, side],
                        f_rs.at[slot, dim, side],
                        toward(dim, step),
                    )
                )
        return made

    def products(t):
        lam = [lam_ref[t, k] for k in range(3)]
        up = []
        down = []
        for dim in range(3):
            up.append(sum(wp[t, dim, k] * lam[k] for k in range(3)))
            down.append(sum(wm[t, dim, k] * lam[k] for k in range(3)))
        x_s[0] = up[0][nx - 1]
        x_s[1] = down[0][0]
        y_s[0] = up[1][:, ny - 1 :, :]
        y_s[1] = down[1][:, :1, :]
        z_s[0] = pack(up[2][:, :, nz - 1 :])
        z_s[1] = pack(down[2][:, :, :1])
        return lam, up, down

    def terms(up, down, slot):
        faces = (x_r, y_r, z_r)
        upper = [ahead(down[dim], dim, faces[dim][slot, 1]) for dim in range(3)]
        lower = [behind(up[dim], dim, faces[dim][slot, 0]) for dim in range(3)]
        return upper, lower

    def sweep(t, n_face, n_fault):
        face_slot = lax.rem(n_face, 2)
        slot = lax.rem(n_fault, 2)
        values = gather([lam_ref[t, k] for k in range(3)])
        sent = sum(
            fault_coef[3 * t + k : 3 * t + k + 1, :] * values[k] for k in range(3)
        )
        for p in range(peers):
            c_s[p] = sent[:, p * slots : (p + 1) * slots]
        copies = []
        for offset in range(1, peers):
            other = lax.rem(me + offset, peers)
            copy = remote(
                c_s.at[other],
                c_r.at[slot, me],
                c_ss.at[offset],
                c_rs.at[slot, offset],
                peer(offset),
            )
            copy.start()
            copies.append(copy)
        lam, up, down = products(t)
        faces = face_copies(face_slot)
        for copy in faces:
            copy.start()
        for copy in faces:
            copy.wait()
        upper, lower = terms(up, down, face_slot)
        coupling = upper[0] + lower[0] + upper[1] + lower[1] + upper[2] + lower[2]
        for copy in copies:
            copy.wait()
        arrived = jnp.concatenate([c_r[slot, p] for p in range(peers)], axis=1)
        hot = row_hot[:rows]
        both = jnp.concatenate(
            [hot * jnp.broadcast_to(part, hot.shape) for part in split_bf16(arrived)], axis=0
        )
        added = lax.dot_general(
            both,
            z_hot[...],
            (((1,), (1,)), ((), ())),
            preferred_element_type=jnp.float32,
        )
        coupling = coupling + (added[:rows] + added[rows:]).reshape(shape)
        relax(t, coupling)

    log_perm = explicit_sum
    for turn, t in enumerate((1, 0)):
        if t == 1:
            relax(1, None)

        def body(step, carry, t=t, turn=turn):
            sweep(t, turn * ITERS + step, turn * (ITERS - 1) + step)
            return carry

        lax.fori_loop(0, ITERS - 1, body, 0)
        slot = (turn * ITERS + ITERS - 1) % 2
        lam, up, down = products(t)
        faces = face_copies(slot)
        for copy in faces:
            copy.start()
        if t == 0:
            porosity_sum = jnp.zeros(shape, jnp.float32)
            for at in range(2):
                water = saturation_ref[at + 1, 0] - saturation_ref[at, 0]
                oil = saturation_ref[at + 1, 1] - saturation_ref[at, 1]
                porosity_sum = porosity_sum + (
                    lam_ref[at, 0] * water + lam_ref[at, 1] * oil - lam_ref[at, 2] * (water + oil)
                )
        else:
            porosity = porosity_ref[...]
            src[0, 1] += porosity * (lam[0] - lam[2])
            src[0, 2] += porosity * (lam[1] - lam[2])
            relax(0, None)
        for copy in faces:
            copy.wait()
        upper, lower = terms(up, down, slot)
        p_here = pressure_ref[t]
        flux = jnp.zeros(shape, jnp.float32)
        for dim in range(3):
            got = halos[dim][0]
            flux = (
                flux
                + 0.5
                * (p_here - ahead(p_here, dim, got[1, 8 + t]))
                * (up[dim] - upper[dim])
                + 0.5
                * (behind(p_here, dim, got[0, 8 + t]) - p_here)
                * (lower[dim] - down[dim])
            )
        explicit[...] -= flux

    z_boxes = (
        lax.broadcasted_iota(jnp.int32, (nz, nz), 0) // BOX
        == lax.broadcasted_iota(jnp.int32, (nz, nz), 1)
    ).astype(jnp.float32)
    n_boxes = nx * ny // BOX**2
    xy_boxes = (
        lax.broadcasted_iota(jnp.int32, (n_boxes, nx // BOX * ny), 1) // BOX
        == lax.broadcasted_iota(jnp.int32, (n_boxes, nx // BOX * ny), 0)
    ).astype(jnp.float32)
    boxes = []
    for field in (explicit[...], -porosity_sum):
        in_x = jnp.sum(field.reshape(nx // BOX, BOX, ny, nz), axis=1)
        in_z = jnp.dot(
            in_x.reshape(nx // BOX * ny, nz),
            z_boxes,
            precision=HIGHEST,
            preferred_element_type=jnp.float32,
        )
        boxes.append(
            jnp.dot(xy_boxes, in_z, precision=HIGHEST, preferred_element_type=jnp.float32)
        )
    boxes = jnp.concatenate(boxes, axis=0)[:, : nz // BOX]
    box_row = lax.rem(lax.broadcasted_iota(jnp.int32, boxes.shape, 0), n_boxes)
    share = peers * PARAM_REGIONS
    labels = lax.broadcasted_iota(jnp.int32, (n_gx * share, nz // BOX), 0)
    found = jnp.zeros((4 * n_boxes, n_gx * share), jnp.float32)
    for b in range(n_boxes):
        y_box = b % (ny // BOX)
        region = map_ref[b // (ny // BOX), y_box : y_box + 1, :]
        found = found + lax.dot_general(
            jnp.concatenate(split_bf16(jnp.where(box_row == b, boxes, 0.0)), axis=0),
            (labels == region).astype(jnp.float32).astype(jnp.bfloat16),
            (((1,), (1,)), ((), ())),
            preferred_element_type=jnp.float32,
        )
    found = found[: 2 * n_boxes] + found[2 * n_boxes :]
    for q in range(2):
        of_q = jnp.sum(found[q * n_boxes : (q + 1) * n_boxes], axis=0, keepdims=True)
        for g in range(n_gx):
            g_s[g, q : q + 1, :] = of_q[:, g * share : (g + 1) * share]
    g_copies = []
    for offset in range(1, n_gx):
        copy = remote(
            g_s.at[lax.rem(here[0] + offset, n_gx)],
            g_r.at[offset],
            g_ss.at[offset],
            g_rs.at[offset],
            toward(0, offset),
        )
        copy.start()
        g_copies.append(copy)
    for copy in g_copies:
        copy.wait()
    part = g_s[here[0]]
    for offset in range(1, n_gx):
        part = part + g_r[offset]
    lanes = r_s.shape[2]
    together = lanes // PARAM_REGIONS
    for p in range(peers):
        first = p // together * lanes
        r_s[p] = part[:, first : first + lanes]
    r_copies = []
    for offset in range(1, peers):
        copy = remote(
            r_s.at[lax.rem(me + offset, peers)],
            r_r.at[offset],
            r_ss.at[offset],
            r_rs.at[offset],
            peer(offset),
        )
        copy.start()
        r_copies.append(copy)
    for copy in r_copies:
        copy.wait()
    part = r_s[me]
    for offset in range(1, peers):
        part = part + r_r[offset]
    mine = jnp.full((2, PARAM_REGIONS), lax.rem(me, together), jnp.int32)
    result = jnp.zeros((2, PARAM_REGIONS), jnp.float32)
    for n in range(together):
        result = jnp.where(
            mine == n, part[:, n * PARAM_REGIONS : (n + 1) * PARAM_REGIONS], result
        )
    region_ref[...] = result


def local(
    pressure,
    saturation,
    permeability,
    porosity,
    upwind_flags,
    diag_inverse,
    seismic_obs,
    well_x,
    well_y,
    well_top,
    well_len,
    well_bhp,
    well_obs,
    fault_cell,
    fault_count,
    fault_trans,
    fault_up,
    region_map,
):
    counts = tuple(lax.axis_size(axis) for axis in ("gx", "gy", "gz"))
    nx, ny, nz = permeability.shape
    peers, slots = fault_cell.shape[1:]
    wide = peers * slots
    n_wells = well_x.shape[2]
    hbm = pl.BlockSpec(memory_space=pltpu.HBM)
    vmem = pl.BlockSpec(memory_space=pltpu.VMEM)
    f32 = jnp.float32
    dma = pltpu.SemaphoreType.DMA
    faces = [(2, ny, nz), (2, nx, 1, nz), (2, ny, nz)]
    bundles = [(2, 10, ny, nz), (2, 10, nx, 1, nz), (2, 10, ny, nz)]
    lanes = 128
    share = peers * PARAM_REGIONS
    large = (
        pressure, saturation, permeability, porosity, upwind_flags, diag_inverse, seismic_obs
    )
    scratch = [
        *[pltpu.VMEM(array.shape, array.dtype) for array in large],
        dma((len(large),)),
        pltpu.VMEM((2, 3, 3, nx, ny, nz), f32),
        pltpu.VMEM((2, 3, 3, nx, ny, nz), f32),
        pltpu.VMEM((2, 3, nx, ny, nz), f32),
        pltpu.VMEM((nx, ny, nz), f32),
        pltpu.VMEM((2 * nx * ny, wide), jnp.bfloat16),
        pltpu.VMEM((nz, wide), jnp.bfloat16),
        pltpu.VMEM((8, wide), f32),
        *[pltpu.VMEM(s, f32) for s in bundles],
        *[pltpu.VMEM(s, f32) for s in bundles],
        dma((3, 2)),
        dma((3, 2)),
        pltpu.VMEM((peers, 8, slots), f32),
        pltpu.VMEM((peers, 8, slots), f32),
        dma((peers,)),
        dma((peers,)),
        pltpu.VMEM((n_wells, nz), f32),
        pltpu.VMEM((counts[2], n_wells, nz), f32),
        dma((counts[2],)),
        dma((counts[2],)),
        *[pltpu.VMEM(s, f32) for s in faces],
        *[pltpu.VMEM((2,) + s, f32) for s in faces],
        dma((3, 2)),
        dma((2, 3, 2)),
        pltpu.VMEM((peers, 1, slots), f32),
        pltpu.VMEM((2, peers, 1, slots), f32),
        dma((peers,)),
        dma((2, peers)),
        pltpu.VMEM((counts[0], 2, share), f32),
        pltpu.VMEM((counts[0], 2, share), f32),
        dma((counts[0],)),
        dma((counts[0],)),
        pltpu.VMEM((peers, 2, lanes), f32),
        pltpu.VMEM((peers, 2, lanes), f32),
        dma((peers,)),
        dma((peers,)),
    ]
    return pl.pallas_call(
        functools.partial(kernel, counts),
        out_shape=(
            jax.ShapeDtypeStruct((2, 3, nx, ny, nz), f32),
            jax.ShapeDtypeStruct((2, PARAM_REGIONS), f32),
        ),
        in_specs=[hbm] * 7 + [vmem] * 11,
        out_specs=(vmem, vmem),
        scratch_shapes=scratch,
        compiler_params=pltpu.CompilerParams(
            collective_id=0, has_side_effects=True, vmem_limit_bytes=63 * 2**20
        ),
    )(
        *large,
        well_x,
        well_y,
        well_top,
        well_len,
        well_bhp,
        well_obs,
        fault_cell,
        fault_count,
        fault_trans,
        fault_up,
        region_map,
    )


def solution(mesh):
    placed = (
        P(None, "gx", "gy", "gz"),
        P(None, None, "gx", "gy", "gz"),
        P("gx", "gy", "gz"),
        P("gx", "gy", "gz"),
        P("gx", "gy", "gz"),
        P(None, None, None, "gx", "gy", "gz"),
        P("gx", "gy", "gz"),
        P("gx", "gy", None),
        P("gx", "gy", None),
        P("gx", "gy", None),
        P("gx", "gy", None),
        P(None, "gx", "gy", None),
        P(None, "gx", "gy", None),
        P(("gx", "gy", "gz"), None, None),
        P(("gx", "gy", "gz"), None),
        P(("gx", "gy", "gz"), None, None),
        P(("gx", "gy", "gz"), None, None),
        P("gx", "gy", "gz"),
    )
    return jax.shard_map(
        local,
        mesh=mesh,
        in_specs=placed,
        out_specs=(P(None, None, "gx", "gy", "gz"), P(None, ("gx", "gy", "gz"))),
        check_vma=False,
    )
```

profile of v0, /device:TPU:0, one launch (start us, length us, event | category | flops | bytes accessed | tf_op | source)
XLA Modules:
  0.0 90.0 jit_solution(3050669998386155057)
XLA Ops:
  0.6 86.4 %shard_map.185 = (f32[2,3,16,8,128]{4,3,2,1,0:T(8,128)}, f32[2,32]{1,0:T(2,128)}) custom-call(f32[2,16,8,128]{3,2,1,0:T(8,128)} %pressure_hbm.1, f32[3,2,16,8,128]{4,3,2,1,0:T(8,128)} %saturation_hbm.1, f32[16,8,128]{2,1,0:T(8,128)} %perm_hbm.1, f32[16,8,128]{2,1,0:T(8,128)} %porosity_hbm.1, s32[16,8,128]{2,1,0:T(8,128)} %flags_hbm.1, ...), custom_call_target="tpu_custom_call" | custom-call | tf_op jit(solution)/shard_map/pallas_call | solution.py:697
  87.1 1.8 %copy.22 = f32[2,3,16,8,128]{4,3,2,1,0:T(8,128)} copy(f32[2,3,16,8,128]{4,3,2,1,0:T(8,128)} %get-tuple-element.4) | data formatting | bytes 786432
  88.8 1.2 %copy.23 = f32[2,32]{1,0:T(2,128)} copy(f32[2,32]{1,0:T(2,128)} %get-tuple-element.5) | data formatting | bytes 512
where the time goes:
time: 90.3 us; the launch traced here: 90 us
  Pallas kernels  86.4 us (96%)
  local copies, waits for them, and re-layouts  2.96 us (3%)
    pallas_call x1, Pallas kernels, local(): pl.pallas_call(functools.partial(kernel, counts), out_shape=(jax.ShapeDty...  86.4 us
    unnamed x2, local copies, waits for them, and re-layouts  2.96 us

commit v1 on v0

v1 whole, which is shorter than its diff:
```python
import functools

import jax
import jax.numpy as jnp
from jax import lax
from jax.experimental import pallas as pl
from jax.experimental.pallas import tpu as pltpu
from jax.sharding import PartitionSpec as P

ITERS = 6
BOX = 4
PARAM_REGIONS = 32
LANES = 128
NEAR = 8
MESH = pl.DeviceIdType.MESH

fluid_viscosity = (0.4, 0.5, 1.0)
sigma_sq = 64.0
SIDES = tuple((dim, side) for dim in range(3) for side in range(2))


def phase_mobility(water_sat, oil_sat):
    gas_sat = 1.0 - water_sat - oil_sat
    return [
        water_sat * water_sat / fluid_viscosity[0],
        oil_sat * oil_sat / fluid_viscosity[1],
        gas_sat * gas_sat / fluid_viscosity[2],
    ]


def mobility_slopes(water_sat, oil_sat):
    gas_sat = 1.0 - water_sat - oil_sat
    return (
        2.0 * water_sat / fluid_viscosity[0] - 2.0 * gas_sat / fluid_viscosity[2],
        2.0 * oil_sat / fluid_viscosity[1] - 2.0 * gas_sat / fluid_viscosity[2],
    )


def split(value, parts):
    pieces = []
    for _ in range(parts):
        piece = value.astype(jnp.bfloat16)
        pieces.append(piece)
        value = value - piece.astype(jnp.float32)
    return pieces


def kernel(
    counts,
    pressure_hbm,
    saturation_hbm,
    perm_hbm,
    porosity_hbm,
    flags_hbm,
    inverse_hbm,
    seismic_hbm,
    well_x_ref,
    well_y_ref,
    well_top_ref,
    well_len_ref,
    bhp_ref,
    obs_ref,
    fault_cell_ref,
    fault_count_ref,
    fault_trans_ref,
    fault_up_ref,
    map_ref,
    lam_hbm,
    region_ref,
    pressure_ref,
    sat_ref,
    perm_ref,
    porosity_ref,
    flags_ref,
    inverse_ref,
    seismic_ref,
    in_sem,
    out_sem,
    mob,
    wp,
    wm,
    src,
    explicit,
    lam,
    const,
    lead,
    turn_c,
    turn_d,
    push,
    push_turn_c,
    push_turn_d,
    flux_base,
    flux_lead,
    por,
    total_r,
    delta,
    row_hot,
    z_hot,
    found_hot,
    f_cell,
    f_scale,
    f_up,
    f_tmp,
    f_own,
    f_coef,
    f_send,
    bx_s,
    by_s,
    bz_s,
    bx_r,
    by_r,
    bz_r,
    b_ss,
    b_rs,
    map_r,
    map_ss,
    map_rs,
    m_s,
    m_r,
    m_ss,
    m_rs,
    w_s,
    w_r,
    w_ss,
    w_rs,
    x_s,
    y_s,
    z_s,
    x_r,
    y_r,
    z_r,
    h_ss,
    h_rs,
    v_s,
    v_r,
    v_ss,
    v_rs,
    c_s,
    c_r,
    c_ss,
    c_rs,
    r_s,
    r_r,
    r_ss,
    r_rs,
):
    n_gx, n_gy, n_gz = counts
    here = (lax.axis_index("gx"), lax.axis_index("gy"), lax.axis_index("gz"))
    peers = n_gy * n_gz
    devices = n_gx * peers
    me = here[1] * n_gz + here[2]
    index = here[0] * peers + me
    shape = perm_ref.shape
    nx, ny, nz = shape
    rows = nx * ny
    slots = c_r.shape[2]
    f32 = jnp.float32

    def flip(number, bits):
        bit = 1
        while bit <= bits:
            if bits & bit:
                number = number + bit - 2 * bit * lax.rem(number // bit, 2)
            bit *= 2
        return number

    def peer(order):
        return (here[0], flip(here[1], order // n_gz), flip(here[2], order % n_gz))

    def peer_place(order):
        other = peer(order)
        return other[1] * n_gz + other[2]

    def toward(dim, step):
        moved = list(here)
        moved[dim] = lax.rem(here[dim] + step + counts[dim], counts[dim])
        return tuple(moved)

    def device(number):
        return (number // peers, lax.rem(number, peers) // n_gz, lax.rem(number, n_gz))

    def remote(source, target, send, recv, to):
        return pltpu.make_async_remote_copy(
            src_ref=source,
            dst_ref=target,
            send_sem=send,
            recv_sem=recv,
            device_id=to,
            device_id_type=MESH,
        )

    has_next = [here[dim] < counts[dim] - 1 for dim in range(3)]
    has_last = [here[dim] > 0 for dim in range(3)]

    def sends(dim, side):
        return has_next[dim] if side == 0 else has_last[dim]

    def receives(dim, side):
        return has_last[dim] if side == 0 else has_next[dim]

    loads = [
        pltpu.make_async_copy(source, target, in_sem.at[n])
        for n, (source, target) in enumerate(
            (
                (saturation_hbm, sat_ref),
                (perm_hbm, perm_ref),
                (pressure_hbm, pressure_ref),
                (flags_hbm, flags_ref),
                (seismic_hbm, seismic_ref),
                (inverse_hbm, inverse_ref),
                (porosity_hbm, porosity_ref),
            )
        )
    ]
    for load in loads:
        load.start()
    for ref in (bx_r, by_r, bz_r, x_r, y_r, z_r, m_r, v_r, c_r, map_r):
        ref[...] = jnp.zeros_like(ref)

    barrier = pltpu.get_barrier_semaphore()
    for offset in range(1, devices):
        pl.semaphore_signal(
            barrier,
            inc=1,
            device_id=device(lax.rem(index + offset, devices)),
            device_id_type=MESH,
        )

    yi = lax.broadcasted_iota(jnp.int32, shape, 1)
    zi = lax.broadcasted_iota(jnp.int32, shape, 2)
    iotas = (None, yi, zi)
    diagonal = lax.broadcasted_iota(jnp.int32, shape, 0) == zi

    def pack(field, lane):
        return jnp.sum(jnp.where(diagonal, field[:, :, lane : lane + 1], 0.0), axis=0)

    def unpack(tile):
        return jnp.concatenate(
            [jnp.broadcast_to(tile[:, x : x + 1], (ny, nz))[None] for x in range(nx)], axis=0
        )

    def at_next(field, dim, edge):
        if dim == 0:
            return jnp.concatenate([field[1:], edge], axis=0)
        last = shape[dim] - 1
        return jnp.where(iotas[dim] == last, edge, pltpu.roll(field, last, dim))

    def at_last(field, dim, edge):
        if dim == 0:
            return jnp.concatenate([edge, field[:-1]], axis=0)
        return jnp.where(iotas[dim] == 0, edge, pltpu.roll(field, 1, dim))

    def edge_of(dim, halo):
        if dim == 0:
            return halo[None]
        return halo if dim == 1 else unpack(halo)

    def no_edge(dim):
        return jnp.zeros((1, ny, nz), f32) if dim == 0 else 0.0

    def faults_in_order(array, target):
        for order in range(peers):
            target[order : order + 1, :] = array[pl.ds(peer_place(order), 1), :]

    faults_in_order(fault_cell_ref.at[0], f_cell)
    faults_in_order(fault_up_ref.at[0], f_up)
    slot_index = lax.broadcasted_iota(jnp.int32, (1, slots), 1)
    for p in range(peers):
        f_tmp[p : p + 1, :] = jnp.where(
            slot_index < fault_count_ref[:, p : p + 1], fault_trans_ref[0, p : p + 1, :], 0.0
        )
    faults_in_order(f_tmp, f_scale)
    f_row = f_cell[...] // nz
    f_z = f_cell[...] - f_row * nz

    def gather(refs, unroll):
        def body(x, chosen):
            for y in range(ny):
                here_row = f_row == x * ny + y
                chosen = [
                    jnp.where(
                        here_row,
                        jnp.take_along_axis(
                            jnp.broadcast_to(ref[x, y : y + 1, :], (peers, nz)),
                            f_z,
                            axis=1,
                            mode="promise_in_bounds",
                        ),
                        value,
                    )
                    for ref, value in zip(refs, chosen)
                ]
            return chosen

        start = [jnp.zeros((peers, slots), f32) for _ in refs]
        return lax.fori_loop(0, nx, body, start, unroll=unroll)

    loads[0].wait()
    mobility = [phase_mobility(sat_ref[t + 1, 0], sat_ref[t + 1, 1]) for t in range(2)]
    for t in range(2):
        for k in range(3):
            mob[t, k] = mobility[t][k]
    for load in loads[1:4]:
        load.wait()
    perm = perm_ref[...]

    def bundle(part, fields):
        for q, field in enumerate(fields):
            bx_s[part, 0, q] = field[nx - 1]
            bx_s[part, 1, q] = field[0]
            by_s[part, 0, q] = field[:, ny - 1 :, :]
            by_s[part, 1, q] = field[:, :1, :]
            bz_s[part, 0, q] = pack(field, nz - 1)
            bz_s[part, 1, q] = pack(field, 0)

    def bundle_copy(part, dim, side):
        sent, got = ((bx_s, bx_r), (by_s, by_r), (bz_s, bz_r))[dim]
        return remote(
            sent.at[part, side],
            got.at[part, side],
            b_ss.at[part, dim, side],
            b_rs.at[part, dim, side],
            toward(dim, 1 - 2 * side),
        )

    def map_copy(dim, side):
        return remote(
            map_ref,
            map_r.at[2 * dim + side],
            map_ss.at[dim, side],
            map_rs.at[dim, side],
            toward(dim, 1 - 2 * side),
        )

    def start_faces(copies):
        for dim, side in SIDES:

            @pl.when(sends(dim, side))
            def _():
                for copy in copies:
                    copy(dim, side).start()

    def wait_faces(copies):
        for dim, side in SIDES:

            @pl.when(sends(dim, side))
            def _():
                for copy in copies:
                    copy(dim, side).wait_send()

            @pl.when(receives(dim, side))
            def _():
                for copy in copies:
                    copy(dim, side).wait_recv()

    bundle(0, [perm] + mobility[1] + [flags_ref[...].astype(f32)])

    n_wells = well_top_ref.shape[2]
    eye = lax.broadcasted_iota(jnp.int32, (n_wells, n_wells), 0) == lax.broadcasted_iota(
        jnp.int32, (n_wells, n_wells), 1
    )

    def as_column(row):
        return jnp.sum(jnp.where(eye, row.astype(f32), 0.0), axis=1, keepdims=True)

    def as_row(column):
        return jnp.sum(jnp.where(eye, column, 0.0), axis=0, keepdims=True)

    well_row = well_x_ref[0] * ny + well_y_ref[0]
    well_hot = (
        (
            lax.broadcasted_iota(jnp.int32, (n_wells, rows), 1).astype(f32) == as_column(well_row)
        )
        .astype(f32)
        .astype(jnp.bfloat16)
    )
    well_hot_t = (lax.broadcasted_iota(jnp.int32, (rows, n_wells), 0) == well_row).astype(f32)
    depth = (here[2] * nz + lax.broadcasted_iota(jnp.int32, (n_wells, nz), 1)).astype(f32)
    top = as_column(well_top_ref[0])
    bottom = as_column(well_top_ref[0] + well_len_ref[0])
    perforated = jnp.where((depth >= top) & (depth < bottom), 1.0, 0.0)

    def total(t):
        return perm_ref[...] * (mob[t, 0] + mob[t, 1] + mob[t, 2])

    fields = []
    for t in range(2):
        whole = total(t)
        fields += [
            (whole * pressure_ref[t]).reshape(rows, nz),
            whole.reshape(rows, nz),
        ]
    pieces = jnp.concatenate(split(jnp.concatenate(fields, axis=1), 3), axis=0)
    of_wells = jnp.dot(
        jnp.concatenate([well_hot] * 3, axis=1), pieces, preferred_element_type=f32
    )
    w_s[...] = jnp.zeros_like(w_s)
    for t in range(2):
        bhp = as_column(bhp_ref[t, 0])
        rate = jnp.sum(
            perforated
            * (
                of_wells[:, 2 * t * nz : (2 * t + 1) * nz]
                - bhp * of_wells[:, (2 * t + 1) * nz : (2 * t + 2) * nz]
            ),
            axis=1,
            keepdims=True,
        )
        w_s[t : t + 1, :n_wells] = as_row(rate)

    pl.semaphore_wait(barrier, devices - 1)
    w_copies = []
    for offset in range(1, n_gz):
        copy = remote(
            w_s,
            w_r.at[offset],
            w_ss.at[offset],
            w_rs.at[offset],
            (here[0], here[1], lax.rem(here[2] + offset, n_gz)),
        )
        copy.start()
        w_copies.append(copy)
    start_faces([functools.partial(bundle_copy, 0)])

    def order_far_first():
        return range(peers - 1, 0, -1)

    def group(order):
        return 0 if order < NEAR else 1

    own = gather([mob.at[t, k] for t in (1, 0) for k in range(3)], False)
    for q in range(6):
        f_own[q] = own[q]
        m_s[q] = own[q]
    for order in order_far_first():
        remote(
            m_s.at[:, pl.ds(order, 1)],
            m_r.at[:, pl.ds(order, 1)],
            m_ss,
            m_rs,
            peer(order),
        ).start()

    for order in range(peers):
        lanes = slice(order * slots, (order + 1) * slots)
        row_hot[:, lanes] = (
            (lax.broadcasted_iota(jnp.int32, (rows, slots), 0) == f_row[order : order + 1])
            .astype(f32)
            .astype(jnp.bfloat16)
        )
        z_hot[:, lanes] = (
            (lax.broadcasted_iota(jnp.int32, (nz, slots), 0) == f_z[order : order + 1])
            .astype(f32)
            .astype(jnp.bfloat16)
        )

    def scatter(values, first):
        high, low = split(values, 2)
        marked = []
        for n in range(values.shape[0]):
            order = first + n
            if order == 0:
                continue
            hot = z_hot[:, order * slots : (order + 1) * slots]
            marked.append(
                jnp.concatenate(
                    [hot * jnp.broadcast_to(part[n : n + 1], hot.shape) for part in (high, low)],
                    axis=0,
                )
            )
        start = max(first, 1)
        added = lax.dot_general(
            row_hot[:, start * slots : (first + values.shape[0]) * slots],
            jnp.concatenate(marked, axis=1),
            (((1,), (1,)), ((), ())),
            preferred_element_type=f32,
        )
        return (added[:, :nz] + added[:, nz:]).reshape(shape)

    for load in loads[4:]:
        load.wait()
    for copy in w_copies:
        copy.wait()
    rates = w_s[...]
    for offset in range(1, n_gz):
        rates = rates + w_r[offset]

    def sources(t):
        misfit = (rates[t : t + 1, :n_wells] - obs_ref[t, 0]) / sigma_sq
        weighted = well_hot_t * misfit
        both = jnp.concatenate([weighted, weighted * bhp_ref[t, 0]], axis=0)
        spread = jnp.dot(
            jnp.concatenate(split(both, 3), axis=0),
            perforated.astype(jnp.bfloat16),
            preferred_element_type=f32,
        )
        spread = spread[: 2 * rows] + spread[2 * rows : 4 * rows] + spread[4 * rows :]
        drawn = pressure_ref[t] * spread[:rows].reshape(shape) - spread[rows:].reshape(shape)
        water_slope, oil_slope = mobility_slopes(sat_ref[t + 1, 0], sat_ref[t + 1, 1])
        whole = total(t)
        src[t, 0] = whole * spread[:rows].reshape(shape)
        water_source = perm_ref[...] * drawn * water_slope
        if t == 1:
            water_source = water_source + (sat_ref[2, 0] - seismic_ref[...])
        src[t, 1] = water_source
        src[t, 2] = perm_ref[...] * drawn * oil_slope
        return whole * drawn

    def face_coefficients(t, flags, bits_at, perm_from, mob_from):
        own_flags = flags.astype(jnp.int32)
        for dim in range(3):
            got = (bx_r, by_r, bz_r)[dim]

            def halo(part, side, q):
                return edge_of(dim, got[part, side, q])

            up_face = jnp.sqrt(
                perm_ref[...] * at_next(perm_ref[...], dim, halo(0, 1, 0))
            )
            low_face = jnp.sqrt(
                perm_ref[...] * at_last(perm_ref[...], dim, halo(0, 0, 0))
            )
            up_ok = has_next[dim].astype(f32)
            low_ok = has_last[dim].astype(f32)
            if dim == 0:
                up_face = jnp.concatenate([up_face[:-1], up_face[-1:] * up_ok], axis=0)
                low_face = jnp.concatenate([low_face[:1] * low_ok, low_face[1:]], axis=0)
            else:
                up_face = up_face * jnp.where(iotas[dim] == shape[dim] - 1, up_ok, 1.0)
                low_face = low_face * jnp.where(iotas[dim] == 0, low_ok, 1.0)
            bit = 3 * t + dim
            low_flags = at_last(flags, dim, halo(0, 0, 4)).astype(jnp.int32)
            own_up = jnp.bitwise_and(jnp.right_shift(own_flags, bit), 1) == 1
            low_up = jnp.bitwise_and(jnp.right_shift(low_flags, bit), 1) == 1
            for k in range(3):
                part, q = mob_from(k)
                m = mob[t, k]
                wp[t, dim, k] = up_face * jnp.where(
                    own_up, m, at_next(m, dim, halo(part, 1, q))
                )
                wm[t, dim, k] = low_face * jnp.where(
                    low_up, at_last(m, dim, halo(part, 0, q)), m
                )

    def face_copy(parity, dim, side):
        sent, got = ((x_s, x_r), (y_s, y_r), (z_s, z_r))[dim]
        return remote(
            sent.at[side],
            got.at[parity, side],
            h_ss.at[dim, side],
            h_rs.at[parity, dim, side],
            toward(dim, 1 - 2 * side),
        )

    def send_faces(parity, up, down):
        x_s[0] = up[0][nx - 1]
        x_s[1] = down[0][0]
        y_s[0] = up[1][:, ny - 1 :, :]
        y_s[1] = down[1][:, :1, :]
        z_s[0] = pack(up[2], nz - 1)
        z_s[1] = pack(down[2], 0)
        start_faces([functools.partial(face_copy, parity)])
        inner = at_last(up[0], 0, no_edge(0)) + at_next(down[0], 0, no_edge(0))
        for dim in (1, 2):
            inner = inner + at_last(up[dim], dim, 0.0) + at_next(down[dim], dim, 0.0)
        return inner

    def add_faces(parity, inner):
        wait_faces([functools.partial(face_copy, parity)])
        inner = jnp.concatenate(
            [
                inner[:1] + x_r[parity, 0][None],
                inner[1 : nx - 1],
                inner[nx - 1 :] + x_r[parity, 1][None],
            ],
            axis=0,
        )
        inner = inner + jnp.where(
            yi == 0, y_r[parity, 0], jnp.where(yi == ny - 1, y_r[parity, 1], 0.0)
        )
        return inner + jnp.where(
            zi == 0,
            unpack(z_r[parity, 0]),
            jnp.where(zi == nz - 1, unpack(z_r[parity, 1]), 0.0),
        )

    def fault_copy(parity, low, high, order, to):
        return remote(
            c_s.at[parity, low:high],
            c_r.at[parity, low:high],
            c_ss.at[parity],
            c_rs.at[parity, group(low)],
            to,
        )

    def send_faults(parity, values):
        c_s[parity] = values
        for order in order_far_first():
            fault_copy(parity, order, order + 1, order, peer(order)).start()

    def add_faults(parity, inner):
        fault_copy(parity, 1, NEAR, 1, peer(1)).wait_recv()
        inner = inner + scatter(c_r[parity, :NEAR], 0)
        fault_copy(parity, NEAR, peers, NEAR, peer(NEAR)).wait_recv()
        inner = inner + scatter(c_r[parity, NEAR:], NEAR)
        fault_copy(parity, 1, peers, 1, peer(1)).wait_send()
        return inner

    def scalar_round(parity, t, aside):
        send_faults(parity, f_send[t] * gather([delta], True)[0])
        now = delta[...]
        inner = send_faces(
            parity,
            [push[t, 0, dim] * now for dim in range(3)],
            [push[t, 1, dim] * now for dim in range(3)],
        )
        if aside is not None:
            aside()
        inner = add_faces(parity, inner)
        inner = add_faults(parity, inner)
        delta[...] = inner
        total_r[...] += inner

    def dot3(coefficients, values):
        return sum(coefficients(k) * values(k) for k in range(3))

    def scalar_push(t):
        for dim in range(3):
            push[t, 0, dim] = dot3(lambda k: wp[t, dim, k], lambda k: inverse_ref[t, 0, k])
            push[t, 1, dim] = dot3(lambda k: wm[t, dim, k], lambda k: inverse_ref[t, 0, k])

    def scalar_faults(t):
        values = gather([inverse_ref.at[t, 0, k] for k in range(3)], False)
        f_send[t] = dot3(lambda k: f_coef[t, k], lambda k: values[k])

    explicit[...] = sources(1)
    total_r[...] = src[1, 0]
    for k in range(3):
        const[k] = inverse_ref[1, 1, k] * src[1, 1] + inverse_ref[1, 2, k] * src[1, 2]
        lam[1, k] = const[k] + inverse_ref[1, 0, k] * src[1, 0]
    values = gather([lam.at[1, k] for k in range(3)], True)
    for k in range(3):
        v_s[k] = values[k]

    def vector_copy(low, high, to):
        return remote(
            v_s.at[:, low:high],
            v_r.at[:, low:high],
            v_ss,
            v_rs.at[group(low)],
            to,
        )

    for order in order_far_first():
        vector_copy(order, order + 1, peer(order)).start()
    wait_faces([functools.partial(bundle_copy, 0)])
    flags = flags_ref[...].astype(f32)
    face_coefficients(1, flags, None, None, lambda k: (0, 1 + k))
    inner = send_faces(
        0,
        [dot3(lambda k: wp[1, dim, k], lambda k: lam[1, k]) for dim in range(3)],
        [dot3(lambda k: wm[1, dim, k], lambda k: lam[1, k]) for dim in range(3)],
    )
    bundle(1, [mob[0, k] for k in range(3)] + [pressure_ref[t] for t in range(2)])
    start_faces([functools.partial(bundle_copy, 1), map_copy])
    scalar_push(1)
    m_all = remote(m_s.at[:, 1:], m_r.at[:, 1:], m_ss, m_rs, peer(1))
    m_all.wait()
    for t in range(2):
        own_up = jnp.bitwise_and(jnp.right_shift(f_up[...], t), 1) == 1
        for k in range(3):
            q = 3 * (1 - t) + k
            f_coef[t, k] = f_scale[...] * jnp.where(own_up, f_own[q], m_r[q])
    scalar_faults(1)
    inner = add_faces(0, inner)

    def arrived(low, high):
        return dot3(lambda k: f_coef[1, k, low:high], lambda k: v_r[k, low:high])

    vector_copy(1, NEAR, peer(1)).wait_recv()
    inner = inner + scatter(arrived(0, NEAR), 0)
    vector_copy(NEAR, peers, peer(NEAR)).wait_recv()
    inner = inner + scatter(arrived(NEAR, peers), NEAR)
    vector_copy(1, peers, peer(1)).wait_send()
    delta[...] = inner
    total_r[...] += inner

    def prepare_turn():
        explicit[...] += sources(0)
        wait_faces([functools.partial(bundle_copy, 1), map_copy])
        face_coefficients(0, flags_ref[...].astype(f32), None, None, lambda k: (1, k))
        porosity = porosity_ref[...]
        first = src[0, 1] + porosity * (const[0] - const[2])
        second = src[0, 2] + porosity * (const[1] - const[2])
        d_first = porosity * (inverse_ref[1, 0, 0] - inverse_ref[1, 0, 2])
        d_second = porosity * (inverse_ref[1, 0, 1] - inverse_ref[1, 0, 2])
        for k in range(3):
            turn_c[k] = (
                inverse_ref[0, 0, k] * src[0, 0]
                + inverse_ref[0, 1, k] * first
                + inverse_ref[0, 2, k] * second
            )
            turn_d[k] = inverse_ref[0, 1, k] * d_first + inverse_ref[0, 2, k] * d_second
        for side, w in enumerate((wp, wm)):
            for dim in range(3):
                push_turn_c[side, dim] = dot3(lambda k: w[0, dim, k], lambda k: turn_c[k])
                push_turn_d[side, dim] = dot3(lambda k: w[0, dim, k], lambda k: turn_d[k])
        values = gather([ref.at[k] for ref in (turn_c, turn_d) for k in range(3)], False)
        f_send[2] = dot3(lambda k: f_coef[0, k], lambda k: values[k])
        f_send[3] = dot3(lambda k: f_coef[0, k], lambda k: values[3 + k])

    n_rounds = ITERS - 1
    scalar_round(1, 1, prepare_turn)

    def more(t):
        def body(step, carry):
            scalar_round(lax.rem(step, 2), t, None)
            return carry

        return body

    lax.fori_loop(2, n_rounds, more(1), 0)

    out_late = pltpu.make_async_copy(lam.at[1], lam_hbm.at[1], out_sem.at[1])
    out_early = pltpu.make_async_copy(lam.at[0], lam_hbm.at[0], out_sem.at[0])
    parity = n_rounds % 2
    send_faults(parity, f_send[2] + f_send[3] * gather([total_r], True)[0])
    now = total_r[...]
    inner = send_faces(
        parity,
        [push_turn_c[0, dim] + push_turn_d[0, dim] * now for dim in range(3)],
        [push_turn_c[1, dim] + push_turn_d[1, dim] * now for dim in range(3)],
    )
    for k in range(3):
        lam[1, k] = const[k] + inverse_ref[1, 0, k] * total_r[...]
    out_late.start()
    porosity = porosity_ref[...]
    first = src[0, 1] + porosity * (lam[1, 0] - lam[1, 2])
    second = src[0, 2] + porosity * (lam[1, 1] - lam[1, 2])
    for k in range(3):
        const[k] = inverse_ref[0, 1, k] * first + inverse_ref[0, 2, k] * second
    scalar_push(0)
    scalar_faults(0)
    inner = add_faces(parity, inner)
    inner = add_faults(parity, inner)
    delta[...] = inner
    total_r[...] = src[0, 0] + inner

    n_bx, n_by, n_bz = nx // BOX, ny // BOX, nz // BOX
    n_boxes = n_bx * n_by
    wide = n_boxes * n_bz

    def prepare_gradient():
        for dim in range(3):
            got = (bx_r, by_r, bz_r)[dim]
            flux_base[0, dim] = jnp.zeros(shape, f32)
            flux_base[1, dim] = jnp.zeros(shape, f32)
            for t in range(2):
                p_here = pressure_ref[t]
                up_p = 0.5 * (
                    p_here - at_next(p_here, dim, edge_of(dim, got[1, 1, 3 + t]))
                )
                down_p = -0.5 * (
                    at_last(p_here, dim, edge_of(dim, got[1, 0, 3 + t])) - p_here
                )
                source = (lambda k: const[k]) if t == 0 else (lambda k: lam[1, k])
                flux_base[0, dim] += up_p * dot3(lambda k: wp[t, dim, k], source)
                flux_base[1, dim] += down_p * dot3(lambda k: wm[t, dim, k], source)
                if t == 0:
                    flux_lead[0, dim] = up_p * push[0, 0, dim]
                    flux_lead[1, dim] = down_p * push[0, 1, dim]
        steps = []
        for t in range(2):
            water = sat_ref[t + 1, 0] - sat_ref[t, 0]
            oil = sat_ref[t + 1, 1] - sat_ref[t, 1]
            steps.append((water, oil, water + oil))
        por[0] = -(
            lam[1, 0] * steps[1][0]
            + lam[1, 1] * steps[1][1]
            - lam[1, 2] * steps[1][2]
            + const[0] * steps[0][0]
            + const[1] * steps[0][1]
            - const[2] * steps[0][2]
        )
        por[1] = -(
            inverse_ref[0, 0, 0] * steps[0][0]
            + inverse_ref[0, 0, 1] * steps[0][1]
            - inverse_ref[0, 0, 2] * steps[0][2]
        )
        z_lane = lax.broadcasted_iota(jnp.int32, (1, n_bz), 1)

        def own_map(bx, by):
            return map_ref[bx, by : by + 1, :]

        def other_map(dim, side, bx, by):
            return map_r[2 * dim + side, bx, by : by + 1, :]

        labels = [[], [], []]
        for bx in range(n_bx):
            for by in range(n_by):
                labels[0].append(own_map(bx, by))
                labels[1].append(
                    other_map(1, 0, bx, n_by - 1) if by == 0 else other_map(1, 1, bx, 0)
                )
                if bx == 0:
                    label = other_map(0, 0, n_bx - 1, by)
                elif bx == n_bx - 1:
                    label = other_map(0, 1, 0, by)
                else:
                    even, odd = 2 * (bx - 1), 2 * (bx - 1) + 1
                    label = jnp.zeros((1, n_bz), jnp.int32)
                    for lane, side, box in (
                        (0, 0, even),
                        (1, 0, odd),
                        (n_bz - 2, 1, odd),
                        (n_bz - 1, 1, even),
                    ):
                        edge = n_bz - 1 if side == 0 else 0
                        label = jnp.where(
                            z_lane == lane,
                            other_map(2, side, box, by)[:, edge : edge + 1],
                            label,
                        )
                labels[2].append(label)
        n_regions = devices * PARAM_REGIONS
        for part in range(3):
            label = jnp.concatenate(labels[part], axis=1)
            found_hot[:, part * wide : (part + 1) * wide] = (
                (lax.broadcasted_iota(jnp.int32, (n_regions, wide), 0) == label)
                .astype(f32)
                .astype(jnp.bfloat16)
            )

    parity = (n_rounds + 1) % 2
    scalar_round(parity, 0, prepare_gradient)
    lax.fori_loop(n_rounds + 2, 2 * n_rounds, more(0), 0)

    now = total_r[...]
    flux = [
        [flux_base[side, dim] + flux_lead[side, dim] * now for dim in range(3)]
        for side in range(2)
    ]
    gradient = explicit[...]
    for dim in range(3):
        gradient = gradient - (
            flux[0][dim]
            + flux[1][dim]
            + at_last(flux[0][dim], dim, no_edge(dim))
            + at_next(flux[1][dim], dim, no_edge(dim))
        )

    def x_sums(field):
        return jnp.sum(field.reshape(n_bx, BOX, ny, nz), axis=1)

    y_pushed = x_sums(jnp.where(yi == 0, flux[1][1], 0.0) + jnp.where(yi == ny - 1, flux[0][1], 0.0))
    z_pushed = x_sums(jnp.where(zi == 0, flux[1][2], 0.0) + jnp.where(zi == nz - 1, flux[0][2], 0.0))
    lane = lax.broadcasted_iota(jnp.int32, (ny, nz), 1)

    def moved(tile):
        return jnp.where(
            lane == BOX,
            pltpu.roll(tile, BOX, 1),
            jnp.where(lane == nz - 1 - BOX, pltpu.roll(tile, nz - BOX, 1), 0.0),
        )

    mixed = jnp.concatenate(
        [flux[1][0][0][None]]
        + [(z_pushed[2 * n] + moved(z_pushed[2 * n + 1]))[None] for n in range(n_bx // 2)]
        + [flux[0][0][nx - 1][None]],
        axis=0,
    )
    stacked = jnp.concatenate(
        [x_sums(gradient), x_sums(por[0] + por[1] * now), -y_pushed, -mixed], axis=0
    ).reshape(4 * n_bx * ny, nz)
    z_boxes = (
        (
            lax.broadcasted_iota(jnp.int32, (nz, wide), 0) // BOX
            == lax.rem(lax.broadcasted_iota(jnp.int32, (nz, wide), 1), n_bz)
        )
        .astype(f32)
        .astype(jnp.bfloat16)
    )
    boxed = jnp.dot(
        jnp.concatenate(split(stacked, 2), axis=1),
        jnp.concatenate([z_boxes] * 2, axis=0),
        preferred_element_type=f32,
    )
    in_box = (
        lax.broadcasted_iota(jnp.int32, (n_bx * ny, wide), 1) // n_bz
        == lax.broadcasted_iota(jnp.int32, (n_bx * ny, wide), 0) // BOX
    )
    sums = [
        jnp.sum(
            jnp.where(in_box, boxed[n * n_bx * ny : (n + 1) * n_bx * ny], 0.0),
            axis=0,
            keepdims=True,
        )
        for n in range(4)
    ]
    none = jnp.zeros((1, wide), f32)
    perm_row = jnp.concatenate([sums[0], sums[2], sums[3]], axis=1)
    por_row = jnp.concatenate([sums[1], none, none], axis=1)
    parts = [
        part.astype(f32) for row in (perm_row, por_row) for part in split(row, 2)
    ]
    which = lax.broadcasted_iota(jnp.int32, (8, 3 * wide), 0)
    lines = jnp.zeros((8, 3 * wide), f32)
    for n, part in enumerate(parts):
        lines = jnp.where(which == n, part, lines)
    found = lax.dot_general(
        lines.astype(jnp.bfloat16),
        found_hot[...],
        (((1,), (1,)), ((), ())),
        preferred_element_type=f32,
    )
    together = LANES // PARAM_REGIONS
    for n in range(devices // together):
        lanes = slice(n * LANES, (n + 1) * LANES)
        r_s[n, 0:1] = found[0:1, lanes] + found[1:2, lanes]
        r_s[n, 1:2] = found[2:3, lanes] + found[3:4, lanes]
    r_copies = []
    for offset in range(1, devices):
        other = lax.rem(index + offset, devices)
        copy = remote(
            r_s.at[other // together],
            r_r.at[offset],
            r_ss.at[offset],
            r_rs.at[offset],
            device(other),
        )
        copy.start()
        r_copies.append(copy)
    for k in range(3):
        lam[0, k] = const[k] + inverse_ref[0, 0, k] * total_r[...]
    out_early.start()
    part = r_s[index // together]
    for offset, copy in enumerate(r_copies):
        copy.wait_recv()
        part = part + r_r[offset + 1]
    mine = jnp.full((2, PARAM_REGIONS), lax.rem(index, together), jnp.int32)
    result = jnp.zeros((2, PARAM_REGIONS), f32)
    for n in range(together):
        result = jnp.where(
            mine == n, part[:, n * PARAM_REGIONS : (n + 1) * PARAM_REGIONS], result
        )
    region_ref[...] = result
    for copy in r_copies:
        copy.wait_send()
    out_late.wait()
    out_early.wait()


def local(*arrays):
    (
        pressure,
        saturation,
        permeability,
        porosity,
        upwind_flags,
        diag_inverse,
        seismic_obs,
        well_x,
        well_y,
        well_top,
        well_len,
        well_bhp,
        well_obs,
        fault_cell,
        fault_count,
        fault_trans,
        fault_up,
        region_map,
    ) = arrays
    counts = tuple(lax.axis_size(axis) for axis in ("gx", "gy", "gz"))
    nx, ny, nz = permeability.shape
    peers, slots = fault_cell.shape[1:]
    devices = counts[0] * peers
    hbm = pl.BlockSpec(memory_space=pltpu.HBM)
    vmem = pl.BlockSpec(memory_space=pltpu.VMEM)
    f32 = jnp.float32
    bf16 = jnp.bfloat16
    dma = pltpu.SemaphoreType.DMA

    def field(*lead, dtype=f32):
        return pltpu.VMEM(lead + (nx, ny, nz), dtype)

    def per_fault(*lead, dtype=f32):
        return pltpu.VMEM(lead + (peers, slots), dtype)

    bundles = [(2, 2, 5, ny, nz), (2, 2, 5, nx, 1, nz), (2, 2, 5, ny, nz)]
    faces = [(2, ny, nz), (2, nx, 1, nz), (2, ny, nz)]
    large = arrays[:7]
    scratch = [
        *[pltpu.VMEM(array.shape, array.dtype) for array in large],
        dma((len(large),)),
        dma((2,)),
        field(2, 3),
        field(2, 3, 3),
        field(2, 3, 3),
        field(2, 3),
        field(),
        field(2, 3),
        field(3),
        field(1),
        field(3),
        field(3),
        field(2, 2, 3),
        field(2, 3),
        field(2, 3),
        field(2, 3),
        field(2, 3),
        field(2),
        field(),
        field(),
        pltpu.VMEM((nx * ny, peers * slots), bf16),
        pltpu.VMEM((nz, peers * slots), bf16),
        pltpu.VMEM((devices * PARAM_REGIONS, 3 * region_map.size), bf16),
        per_fault(dtype=jnp.int32),
        per_fault(),
        per_fault(dtype=jnp.int32),
        per_fault(),
        per_fault(6),
        per_fault(2, 3),
        per_fault(4),
        *[pltpu.VMEM(s, f32) for s in bundles],
        *[pltpu.VMEM(s, f32) for s in bundles],
        dma((2, 3, 2)),
        dma((2, 3, 2)),
        pltpu.VMEM((6,) + region_map.shape, jnp.int32),
        dma((3, 2)),
        dma((3, 2)),
        per_fault(6),
        per_fault(6),
        dma,
        dma,
        pltpu.VMEM((8, LANES), f32),
        pltpu.VMEM((counts[2], 8, LANES), f32),
        dma((counts[2],)),
        dma((counts[2],)),
        *[pltpu.VMEM(s, f32) for s in faces],
        *[pltpu.VMEM((2,) + s, f32) for s in faces],
        dma((3, 2)),
        dma((2, 3, 2)),
        per_fault(3),
        per_fault(3),
        dma,
        dma((2,)),
        per_fault(2),
        per_fault(2),
        dma((2,)),
        dma((2, 2)),
        pltpu.VMEM((devices * PARAM_REGIONS // LANES, 2, LANES), f32),
        pltpu.VMEM((devices, 2, LANES), f32),
        dma((devices,)),
        dma((devices,)),
    ]
    return pl.pallas_call(
        functools.partial(kernel, counts),
        out_shape=(
            jax.ShapeDtypeStruct((2, 3, nx, ny, nz), f32),
            jax.ShapeDtypeStruct((2, PARAM_REGIONS), f32),
        ),
        in_specs=[hbm] * 7 + [vmem] * 11,
        out_specs=(hbm, vmem),
        scratch_shapes=scratch,
        compiler_params=pltpu.CompilerParams(
            collective_id=0, has_side_effects=True, vmem_limit_bytes=60 * 2**20
        ),
    )(*arrays)


def solution(mesh):
    cells = P("gx", "gy", "gz")
    column = P("gx", "gy", None)
    every = ("gx", "gy", "gz")
    placed = (
        P(None, "gx", "gy", "gz"),
        P(None, None, "gx", "gy", "gz"),
        cells,
        cells,
        cells,
        P(None, None, None, "gx", "gy", "gz"),
        cells,
        column,
        column,
        column,
        column,
        P(None, "gx", "gy", None),
        P(None, "gx", "gy", None),
        P(every, None, None),
        P(every, None),
        P(every, None, None),
        P(every, None, None),
        cells,
    )
    return jax.shard_map(
        local,
        mesh=mesh,
        in_specs=placed,
        out_specs=(P(None, None, "gx", "gy", "gz"), P(None, every)),
        check_vma=False,
    )
```

time: 90.3 us -> 71.4 us (0.79)
  Pallas kernels: 86.4 us -> 67.5 us
    pallas_call x1, Pallas kernels: 86.4 us -> 67.5 us  [local(): pl.pallas_call(functools.partial(kernel, counts), out_shape=(jax.ShapeDty...]
where the time goes in v1:
time: 71.4 us; the launch traced here: 71.1 us
  Pallas kernels  67.5 us (95%)
  local copies, waits for them, and re-layouts  2.96 us (4%)
    pallas_call x1, Pallas kernels, local(): pl.pallas_call(functools.partial(kernel, counts), out_shape=(jax.ShapeDty...  67.5 us
    unnamed x2, local copies, waits for them, and re-layouts  2.96 us

profile of v1, /device:TPU:0, one launch (start us, length us, event | category | flops | bytes accessed | tf_op | source)
XLA Modules:
  0.0 71.1 jit_solution(8530100410852706065)
XLA Ops:
  0.6 67.5 %shard_map.185 = (f32[2,3,16,8,128]{4,3,2,1,0:T(8,128)}, f32[2,32]{1,0:T(2,128)}) custom-call(f32[2,16,8,128]{3,2,1,0:T(8,128)} %pressure_hbm.1, f32[3,2,16,8,128]{4,3,2,1,0:T(8,128)} %saturation_hbm.1, f32[16,8,128]{2,1,0:T(8,128)} %perm_hbm.1, f32[16,8,128]{2,1,0:T(8,128)} %porosity_hbm.1, s32[16,8,128]{2,1,0:T(8,128)} %flags_hbm.1, ...), custom_call_target="tpu_custom_call" | custom-call | tf_op jit(solution)/shard_map/pallas_call | solution.py:1057
  68.2 1.8 %copy.22 = f32[2,3,16,8,128]{4,3,2,1,0:T(8,128)} copy(f32[2,3,16,8,128]{4,3,2,1,0:T(8,128)} %get-tuple-element.4) | data formatting | bytes 786432
  69.9 1.2 %copy.23 = f32[2,32]{1,0:T(2,128)} copy(f32[2,32]{1,0:T(2,128)} %get-tuple-element.5) | data formatting | bytes 512

commit v2 on v1

--- a/solution.py
+++ b/solution.py
@@ -11,7 +11,7 @@
 BOX = 4
 PARAM_REGIONS = 32
 LANES = 128
-NEAR = 8
+CUTS = (1, 8, 12, 16)
 MESH = pl.DeviceIdType.MESH
 
 fluid_viscosity = (0.4, 0.5, 1.0)
@@ -273,6 +273,22 @@
     f_row = f_cell[...] // nz
     f_z = f_cell[...] - f_row * nz
 
+    def gather_half(ref, low, high):
+        row, at = f_row[low:high], f_z[low:high]
+
+        def body(x, chosen):
+            for y in range(ny):
+                taken = jnp.take_along_axis(
+                    jnp.broadcast_to(ref[x, y : y + 1, :], (high - low, nz)),
+                    at,
+                    axis=1,
+                    mode="promise_in_bounds",
+                )
+                chosen = jnp.where(row == x * ny + y, taken, chosen)
+            return chosen
+
+        return lax.fori_loop(0, nx, body, jnp.zeros((high - low, slots), f32), unroll=True)
+
     def gather(refs, unroll):
         def body(x, chosen):
             for y in range(ny):
@@ -425,8 +441,10 @@
     def order_far_first():
         return range(peers - 1, 0, -1)
 
+    groups = list(zip(CUTS[:-1], CUTS[1:]))
+
     def group(order):
-        return 0 if order < NEAR else 1
+        return [low <= order < high for low, high in groups].index(True)
 
     own = gather([mob.at[t, k] for t in (1, 0) for k in range(3)], False)
     for q in range(6):
@@ -448,34 +466,28 @@
             .astype(f32)
             .astype(jnp.bfloat16)
         )
-        z_hot[:, lanes] = (
+        z_hot[lanes, :] = (
             (lax.broadcasted_iota(jnp.int32, (nz, slots), 0) == f_z[order : order + 1])
             .astype(f32)
-            .astype(jnp.bfloat16)
-        )
-
-    def scatter(values, first):
-        high, low = split(values, 2)
-        marked = []
-        for n in range(values.shape[0]):
-            order = first + n
-            if order == 0:
-                continue
-            hot = z_hot[:, order * slots : (order + 1) * slots]
-            marked.append(
-                jnp.concatenate(
-                    [hot * jnp.broadcast_to(part[n : n + 1], hot.shape) for part in (high, low)],
-                    axis=0,
-                )
-            )
-        start = max(first, 1)
+            .T.astype(jnp.bfloat16)
+        )
+
+    def scatter(read, start, stop):
+        base = start // 4 * 4
+        parts = split(read(base, stop), 2)
+        marked = [[], []]
+        for order in range(start, stop):
+            hot = row_hot[:, order * slots : (order + 1) * slots]
+            at = order - base
+            for pieces, part in zip(marked, parts):
+                pieces.append(hot * jnp.broadcast_to(part[at : at + 1], hot.shape))
         added = lax.dot_general(
-            row_hot[:, start * slots : (first + values.shape[0]) * slots],
-            jnp.concatenate(marked, axis=1),
-            (((1,), (1,)), ((), ())),
+            jnp.concatenate([jnp.concatenate(pieces, axis=1) for pieces in marked], axis=0),
+            z_hot[start * slots : stop * slots, :],
+            (((1,), (0,)), ((), ())),
             preferred_element_type=f32,
         )
-        return (added[:, :nz] + added[:, nz:]).reshape(shape)
+        return (added[:rows] + added[rows:]).reshape(shape)
 
     for load in loads[4:]:
         load.wait()
@@ -593,21 +605,28 @@
             to,
         )
 
-    def send_faults(parity, values):
-        c_s[parity] = values
-        for order in order_far_first():
-            fault_copy(parity, order, order + 1, order, peer(order)).start()
+    def send_faults(parity, ref, lead, fixed):
+        for low in range(peers - 8, -8, -8):
+            part = slice(low, low + 8)
+            values = f_send[lead, part] * gather_half(ref, low, low + 8)
+            if fixed is not None:
+                values = values + f_send[fixed, part]
+            c_s[parity, part] = values
+            for order in range(low + 7, max(low, 1) - 1, -1):
+                fault_copy(parity, order, order + 1, order, peer(order)).start()
 
     def add_faults(parity, inner):
-        fault_copy(parity, 1, NEAR, 1, peer(1)).wait_recv()
-        inner = inner + scatter(c_r[parity, :NEAR], 0)
-        fault_copy(parity, NEAR, peers, NEAR, peer(NEAR)).wait_recv()
-        inner = inner + scatter(c_r[parity, NEAR:], NEAR)
+        def read(low, high):
+            return c_r[parity, low:high]
+
+        for low, high in groups:
+            fault_copy(parity, low, high, low, peer(low)).wait_recv()
+            inner = inner + scatter(read, low, high)
         fault_copy(parity, 1, peers, 1, peer(1)).wait_send()
         return inner
 
     def scalar_round(parity, t, aside):
-        send_faults(parity, f_send[t] * gather([delta], True)[0])
+        send_faults(parity, delta, t, None)
         now = delta[...]
         inner = send_faces(
             parity,
@@ -677,10 +696,9 @@
     def arrived(low, high):
         return dot3(lambda k: f_coef[1, k, low:high], lambda k: v_r[k, low:high])
 
-    vector_copy(1, NEAR, peer(1)).wait_recv()
-    inner = inner + scatter(arrived(0, NEAR), 0)
-    vector_copy(NEAR, peers, peer(NEAR)).wait_recv()
-    inner = inner + scatter(arrived(NEAR, peers), NEAR)
+    for low, high in groups:
+        vector_copy(low, high, peer(low)).wait_recv()
+        inner = inner + scatter(arrived, low, high)
     vector_copy(1, peers, peer(1)).wait_send()
     delta[...] = inner
     total_r[...] += inner
@@ -724,7 +742,7 @@
     out_late = pltpu.make_async_copy(lam.at[1], lam_hbm.at[1], out_sem.at[1])
     out_early = pltpu.make_async_copy(lam.at[0], lam_hbm.at[0], out_sem.at[0])
     parity = n_rounds % 2
-    send_faults(parity, f_send[2] + f_send[3] * gather([total_r], True)[0])
+    send_faults(parity, total_r, 3, 2)
     now = total_r[...]
     inner = send_faces(
         parity,
@@ -918,25 +936,24 @@
         lanes = slice(n * LANES, (n + 1) * LANES)
         r_s[n, 0:1] = found[0:1, lanes] + found[1:2, lanes]
         r_s[n, 1:2] = found[2:3, lanes] + found[3:4, lanes]
-    r_copies = []
-    for offset in range(1, devices):
-        other = lax.rem(index + offset, devices)
-        copy = remote(
+    for order in sorted(range(1, devices), key=lambda n: (-(n % peers // n_gz), -n)):
+        to = (flip(here[0], order // peers),) + peer(order % peers)[1:]
+        other = to[0] * peers + to[1] * n_gz + to[2]
+        remote(
             r_s.at[other // together],
-            r_r.at[offset],
-            r_ss.at[offset],
-            r_rs.at[offset],
-            device(other),
-        )
-        copy.start()
-        r_copies.append(copy)
+            r_r.at[order],
+            r_ss,
+            r_rs,
+            to,
+        ).start()
     for k in range(3):
         lam[0, k] = const[k] + inverse_ref[0, 0, k] * total_r[...]
     out_early.start()
     part = r_s[index // together]
-    for offset, copy in enumerate(r_copies):
-        copy.wait_recv()
-        part = part + r_r[offset + 1]
+    r_all = remote(r_r.at[1:], r_r.at[1:], r_ss, r_rs, peer(1))
+    r_all.wait_recv()
+    for order in range(1, devices):
+        part = part + r_r[order]
     mine = jnp.full((2, PARAM_REGIONS), lax.rem(index, together), jnp.int32)
     result = jnp.zeros((2, PARAM_REGIONS), f32)
     for n in range(together):
@@ -944,8 +961,7 @@
             mine == n, part[:, n * PARAM_REGIONS : (n + 1) * PARAM_REGIONS], result
         )
     region_ref[...] = result
-    for copy in r_copies:
-        copy.wait_send()
+    r_all.wait_send()
     out_late.wait()
     out_early.wait()
 
@@ -1013,7 +1029,7 @@
         field(),
         field(),
         pltpu.VMEM((nx * ny, peers * slots), bf16),
-        pltpu.VMEM((nz, peers * slots), bf16),
+        pltpu.VMEM((peers * slots, nz), bf16),
         pltpu.VMEM((devices * PARAM_REGIONS, 3 * region_map.size), bf16),
         per_fault(dtype=jnp.int32),
         per_fault(),
@@ -1044,22 +1060,23 @@
         per_fault(3),
         per_fault(3),
         dma,
-        dma((2,)),
+        dma((len(CUTS) - 1,)),
         per_fault(2),
         per_fault(2),
         dma((2,)),
-        dma((2, 2)),
+        dma((2, len(CUTS) - 1)),
         pltpu.VMEM((devices * PARAM_REGIONS // LANES, 2, LANES), f32),
         pltpu.VMEM((devices, 2, LANES), f32),
-        dma((devices,)),
-        dma((devices,)),
+        dma,
+        dma,
     ]
-    return pl.pallas_call(
+    results = (
+        jax.ShapeDtypeStruct((2, 3, nx, ny, nz), f32),
+        jax.ShapeDtypeStruct((2, PARAM_REGIONS), f32),
+    )
+    found = pl.pallas_call(
         functools.partial(kernel, counts),
-        out_shape=(
-            jax.ShapeDtypeStruct((2, 3, nx, ny, nz), f32),
-            jax.ShapeDtypeStruct((2, PARAM_REGIONS), f32),
-        ),
+        out_shape=results,
         in_specs=[hbm] * 7 + [vmem] * 11,
         out_specs=(hbm, vmem),
         scratch_shapes=scratch,
@@ -1067,6 +1084,20 @@
             collective_id=0, has_side_effects=True, vmem_limit_bytes=60 * 2**20
         ),
     )(*arrays)
+
+    def finish(lam_ref, region_ref, lam_out, region_out, sem):
+        copy = pltpu.make_async_copy(lam_ref, lam_out, sem)
+        copy.start()
+        region_out[...] = region_ref[...]
+        copy.wait()
+
+    return pl.pallas_call(
+        finish,
+        out_shape=results,
+        in_specs=[vmem, vmem],
+        out_specs=(hbm, vmem),
+        scratch_shapes=[dma],
+    )(*found)
 
 
 def solution(mesh):

time: 71.4 us -> 67.1 us (0.940)
  local copies, waits for them, and re-layouts: 2.96 us -> 0 us
  Pallas kernels: 67.5 us -> 66.2 us
    unnamed x2 -> x0, local copies, waits for them, and re-layouts: 2.96 us -> none
    pallas_call x1 -> x2, Pallas kernels: 67.5 us -> 66.2 us  [the longest x1 63.9 us: local(): pl.pallas_call(functools.partial(kernel, counts), out_shape=results, in_s...]
where the time goes in v2:
time: 67.1 us; the launch traced here: 66.9 us
  Pallas kernels  66.2 us (99%)
    pallas_call x1, Pallas kernels, local(): pl.pallas_call(functools.partial(kernel, counts), out_shape=results, in_s...  63.9 us
    pallas_call x1, Pallas kernels, local(): pl.pallas_call(finish, out_shape=results, in_specs=[vmem, vmem], out_spec...  2.31 us

profile of v2, /device:TPU:0, one launch (start us, length us, event | category | flops | bytes accessed | tf_op | source)
XLA Modules:
  0.0 66.9 jit_solution(3201879940251183375)
XLA Ops:
  0.6 63.9 %shard_map.185 = (f32[2,3,16,8,128]{4,3,2,1,0:T(8,128)}, f32[2,32]{1,0:T(2,128)}) custom-call(f32[2,16,8,128]{3,2,1,0:T(8,128)} %pressure_hbm.1, f32[3,2,16,8,128]{4,3,2,1,0:T(8,128)} %saturation_hbm.1, f32[16,8,128]{2,1,0:T(8,128)} %perm_hbm.1, f32[16,8,128]{2,1,0:T(8,128)} %porosity_hbm.1, s32[16,8,128]{2,1,0:T(8,128)} %flags_hbm.1, ...), custom_call_target="tpu_custom_call" | custom-call | tf_op jit(solution)/shard_map/pallas_call | solution.py:1077
  64.6 2.3 %shard_map.186 = (f32[2,3,16,8,128]{4,3,2,1,0:T(8,128)}, f32[2,32]{1,0:T(2,128)}) custom-call(f32[2,3,16,8,128]{4,3,2,1,0:T(8,128)} %get-tuple-element.4.lam_ref, f32[2,32]{1,0:T(2,128)} %get-tuple-element.5.region_ref), custom_call_target="tpu_custom_call" | custom-call | tf_op jit(solution)/shard_map/pallas_call | solution.py:1094

commit v3 on v2

--- a/solution.py
+++ b/solution.py
@@ -83,7 +83,6 @@
     explicit,
     lam,
     const,
-    lead,
     turn_c,
     turn_d,
     push,
@@ -101,7 +100,6 @@
     f_scale,
     f_up,
     f_tmp,
-    f_own,
     f_coef,
     f_send,
     bx_s,
@@ -289,7 +287,7 @@
 
         return lax.fori_loop(0, nx, body, jnp.zeros((high - low, slots), f32), unroll=True)
 
-    def gather(refs, unroll):
+    def gather(refs):
         def body(x, chosen):
             for y in range(ny):
                 here_row = f_row == x * ny + y
@@ -309,7 +307,7 @@
             return chosen
 
         start = [jnp.zeros((peers, slots), f32) for _ in refs]
-        return lax.fori_loop(0, nx, body, start, unroll=unroll)
+        return lax.fori_loop(0, nx, body, start, unroll=True)
 
     loads[0].wait()
     mobility = [phase_mobility(sat_ref[t + 1, 0], sat_ref[t + 1, 1]) for t in range(2)]
@@ -446,18 +444,25 @@
     def group(order):
         return [low <= order < high for low, high in groups].index(True)
 
-    own = gather([mob.at[t, k] for t in (1, 0) for k in range(3)], False)
-    for q in range(6):
-        f_own[q] = own[q]
-        m_s[q] = own[q]
-    for order in order_far_first():
-        remote(
-            m_s.at[:, pl.ds(order, 1)],
-            m_r.at[:, pl.ds(order, 1)],
-            m_ss,
-            m_rs,
-            peer(order),
-        ).start()
+    def mobility_copy(t, low, high, to):
+        return remote(
+            m_s.at[t, :, low:high], m_r.at[t, :, low:high], m_ss.at[t], m_rs.at[t], to
+        )
+
+    def send_mobility(t):
+        own = gather([mob.at[t, k] for k in range(3)])
+        for k in range(3):
+            m_s[t, k] = own[k]
+        for order in order_far_first():
+            mobility_copy(t, order, order + 1, peer(order)).start()
+
+    def fault_coefficients(t):
+        mobility_copy(t, 1, peers, peer(1)).wait()
+        own_up = jnp.bitwise_and(jnp.right_shift(f_up[...], t), 1) == 1
+        for k in range(3):
+            f_coef[t, k] = f_scale[...] * jnp.where(own_up, m_s[t, k], m_r[t, k])
+
+    send_mobility(1)
 
     for order in range(peers):
         lanes = slice(order * slots, (order + 1) * slots)
@@ -518,7 +523,7 @@
         src[t, 2] = perm_ref[...] * drawn * oil_slope
         return whole * drawn
 
-    def face_coefficients(t, flags, bits_at, perm_from, mob_from):
+    def face_coefficients(t, flags, mob_from):
         own_flags = flags.astype(jnp.int32)
         for dim in range(3):
             got = (bx_r, by_r, bz_r)[dim]
@@ -649,7 +654,7 @@
             push[t, 1, dim] = dot3(lambda k: wm[t, dim, k], lambda k: inverse_ref[t, 0, k])
 
     def scalar_faults(t):
-        values = gather([inverse_ref.at[t, 0, k] for k in range(3)], False)
+        values = gather([inverse_ref.at[t, 0, k] for k in range(3)])
         f_send[t] = dot3(lambda k: f_coef[t, k], lambda k: values[k])
 
     explicit[...] = sources(1)
@@ -657,7 +662,7 @@
     for k in range(3):
         const[k] = inverse_ref[1, 1, k] * src[1, 1] + inverse_ref[1, 2, k] * src[1, 2]
         lam[1, k] = const[k] + inverse_ref[1, 0, k] * src[1, 0]
-    values = gather([lam.at[1, k] for k in range(3)], True)
+    values = gather([lam.at[1, k] for k in range(3)])
     for k in range(3):
         v_s[k] = values[k]
 
@@ -674,7 +679,7 @@
         vector_copy(order, order + 1, peer(order)).start()
     wait_faces([functools.partial(bundle_copy, 0)])
     flags = flags_ref[...].astype(f32)
-    face_coefficients(1, flags, None, None, lambda k: (0, 1 + k))
+    face_coefficients(1, flags, lambda k: (0, 1 + k))
     inner = send_faces(
         0,
         [dot3(lambda k: wp[1, dim, k], lambda k: lam[1, k]) for dim in range(3)],
@@ -683,13 +688,8 @@
     bundle(1, [mob[0, k] for k in range(3)] + [pressure_ref[t] for t in range(2)])
     start_faces([functools.partial(bundle_copy, 1), map_copy])
     scalar_push(1)
-    m_all = remote(m_s.at[:, 1:], m_r.at[:, 1:], m_ss, m_rs, peer(1))
-    m_all.wait()
-    for t in range(2):
-        own_up = jnp.bitwise_and(jnp.right_shift(f_up[...], t), 1) == 1
-        for k in range(3):
-            q = 3 * (1 - t) + k
-            f_coef[t, k] = f_scale[...] * jnp.where(own_up, f_own[q], m_r[q])
+    send_mobility(0)
+    fault_coefficients(1)
     scalar_faults(1)
     inner = add_faces(0, inner)
 
@@ -706,7 +706,7 @@
     def prepare_turn():
         explicit[...] += sources(0)
         wait_faces([functools.partial(bundle_copy, 1), map_copy])
-        face_coefficients(0, flags_ref[...].astype(f32), None, None, lambda k: (1, k))
+        face_coefficients(0, flags_ref[...].astype(f32), lambda k: (1, k))
         porosity = porosity_ref[...]
         first = src[0, 1] + porosity * (const[0] - const[2])
         second = src[0, 2] + porosity * (const[1] - const[2])
@@ -719,16 +719,20 @@
                 + inverse_ref[0, 2, k] * second
             )
             turn_d[k] = inverse_ref[0, 1, k] * d_first + inverse_ref[0, 2, k] * d_second
+
+    def prepare_sends():
+        fault_coefficients(0)
         for side, w in enumerate((wp, wm)):
             for dim in range(3):
                 push_turn_c[side, dim] = dot3(lambda k: w[0, dim, k], lambda k: turn_c[k])
                 push_turn_d[side, dim] = dot3(lambda k: w[0, dim, k], lambda k: turn_d[k])
-        values = gather([ref.at[k] for ref in (turn_c, turn_d) for k in range(3)], False)
+        values = gather([ref.at[k] for ref in (turn_c, turn_d) for k in range(3)])
         f_send[2] = dot3(lambda k: f_coef[0, k], lambda k: values[k])
         f_send[3] = dot3(lambda k: f_coef[0, k], lambda k: values[3 + k])
 
     n_rounds = ITERS - 1
     scalar_round(1, 1, prepare_turn)
+    scalar_round(0, 1, prepare_sends)
 
     def more(t):
         def body(step, carry):
@@ -737,7 +741,7 @@
 
         return body
 
-    lax.fori_loop(2, n_rounds, more(1), 0)
+    lax.fori_loop(3, n_rounds, more(1), 0)
 
     out_late = pltpu.make_async_copy(lam.at[1], lam_hbm.at[1], out_sem.at[1])
     out_early = pltpu.make_async_copy(lam.at[0], lam_hbm.at[0], out_sem.at[0])
@@ -841,13 +845,16 @@
                         )
                 labels[2].append(label)
         n_regions = devices * PARAM_REGIONS
+        region = lax.broadcasted_iota(jnp.int32, (LANES, n_regions), 1).astype(f32)
         for part in range(3):
-            label = jnp.concatenate(labels[part], axis=1)
-            found_hot[:, part * wide : (part + 1) * wide] = (
-                (lax.broadcasted_iota(jnp.int32, (n_regions, wide), 0) == label)
-                .astype(f32)
-                .astype(jnp.bfloat16)
-            )
+            label = jnp.concatenate(labels[part], axis=1).astype(f32)
+            for first in range(0, wide, LANES):
+                column = jnp.broadcast_to(label[:, first : first + LANES], (LANES, LANES)).T
+                found_hot[part * wide + first : part * wide + first + LANES, :] = (
+                    (region == jnp.concatenate([column] * (n_regions // LANES), axis=1))
+                    .astype(f32)
+                    .astype(jnp.bfloat16)
+                )
 
     parity = (n_rounds + 1) % 2
     scalar_round(parity, 0, prepare_gradient)
@@ -925,11 +932,8 @@
     lines = jnp.zeros((8, 3 * wide), f32)
     for n, part in enumerate(parts):
         lines = jnp.where(which == n, part, lines)
-    found = lax.dot_general(
-        lines.astype(jnp.bfloat16),
-        found_hot[...],
-        (((1,), (1,)), ((), ())),
-        preferred_element_type=f32,
+    found = jnp.dot(
+        lines.astype(jnp.bfloat16), found_hot[...], preferred_element_type=f32
     )
     together = LANES // PARAM_REGIONS
     for n in range(devices // together):
@@ -1017,7 +1021,6 @@
         field(),
         field(2, 3),
         field(3),
-        field(1),
         field(3),
         field(3),
         field(2, 2, 3),
@@ -1030,12 +1033,11 @@
         field(),
         pltpu.VMEM((nx * ny, peers * slots), bf16),
         pltpu.VMEM((peers * slots, nz), bf16),
-        pltpu.VMEM((devices * PARAM_REGIONS, 3 * region_map.size), bf16),
+        pltpu.VMEM((3 * region_map.size, devices * PARAM_REGIONS), bf16),
         per_fault(dtype=jnp.int32),
         per_fault(),
         per_fault(dtype=jnp.int32),
         per_fault(),
-        per_fault(6),
         per_fault(2, 3),
         per_fault(4),
         *[pltpu.VMEM(s, f32) for s in bundles],
@@ -1045,10 +1047,10 @@
         pltpu.VMEM((6,) + region_map.shape, jnp.int32),
         dma((3, 2)),
         dma((3, 2)),
-        per_fault(6),
-        per_fault(6),
-        dma,
-        dma,
+        per_fault(2, 3),
+        per_fault(2, 3),
+        dma((2,)),
+        dma((2,)),
         pltpu.VMEM((8, LANES), f32),
         pltpu.VMEM((counts[2], 8, LANES), f32),
         dma((counts[2],)),

time: 67.1 us -> 65.1 us (0.970)
  Pallas kernels: 66.2 us -> 64.1 us
    pallas_call x1, Pallas kernels: 63.9 us -> 61.8 us  [local(): pl.pallas_call(functools.partial(kernel, counts), out_shape=results, in_s...]
where the time goes in v3:
time: 65.1 us; the launch traced here: 64.9 us
  Pallas kernels  64.1 us (98%)
  between operations  0.81 us (1%)
    pallas_call x1, Pallas kernels, local(): pl.pallas_call(functools.partial(kernel, counts), out_shape=results, in_s...  61.8 us
    pallas_call x1, Pallas kernels, local(): pl.pallas_call(finish, out_shape=results, in_specs=[vmem, vmem], out_spec...  2.31 us

profile of v3, /device:TPU:0, one launch (start us, length us, event | category | flops | bytes accessed | tf_op | source)
XLA Modules:
  0.0 64.9 jit_solution(5879605564422885439)
XLA Ops:
  0.6 61.8 %shard_map.185 = (f32[2,3,16,8,128]{4,3,2,1,0:T(8,128)}, f32[2,32]{1,0:T(2,128)}) custom-call(f32[2,16,8,128]{3,2,1,0:T(8,128)} %pressure_hbm.1, f32[3,2,16,8,128]{4,3,2,1,0:T(8,128)} %saturation_hbm.1, f32[16,8,128]{2,1,0:T(8,128)} %perm_hbm.1, f32[16,8,128]{2,1,0:T(8,128)} %porosity_hbm.1, s32[16,8,128]{2,1,0:T(8,128)} %flags_hbm.1, ...), custom_call_target="tpu_custom_call" | custom-call | tf_op jit(solution)/shard_map/pallas_call | solution.py:1079
  62.4 2.3 %shard_map.186 = (f32[2,3,16,8,128]{4,3,2,1,0:T(8,128)}, f32[2,32]{1,0:T(2,128)}) custom-call(f32[2,3,16,8,128]{4,3,2,1,0:T(8,128)} %get-tuple-element.4.lam_ref, f32[2,32]{1,0:T(2,128)} %get-tuple-element.5.region_ref), custom_call_target="tpu_custom_call" | custom-call | tf_op jit(solution)/shard_map/pallas_call | solution.py:1096

commit v4 on v3

--- a/solution.py
+++ b/solution.py
@@ -11,7 +11,7 @@
 BOX = 4
 PARAM_REGIONS = 32
 LANES = 128
-CUTS = (1, 8, 12, 16)
+CUTS = (1, 12, 16)
 MESH = pl.DeviceIdType.MESH
 
 fluid_viscosity = (0.4, 0.5, 1.0)
@@ -54,6 +54,26 @@
     flags_hbm,
     inverse_hbm,
     seismic_hbm,
+    well_x_hbm,
+    well_y_hbm,
+    well_top_hbm,
+    well_len_hbm,
+    bhp_hbm,
+    obs_hbm,
+    fault_cell_hbm,
+    fault_count_hbm,
+    fault_trans_hbm,
+    fault_up_hbm,
+    map_hbm,
+    lam_hbm,
+    region_ref,
+    pressure_ref,
+    sat_ref,
+    perm_ref,
+    porosity_ref,
+    flags_ref,
+    inverse_ref,
+    seismic_ref,
     well_x_ref,
     well_y_ref,
     well_top_ref,
@@ -65,15 +85,6 @@
     fault_trans_ref,
     fault_up_ref,
     map_ref,
-    lam_hbm,
-    region_ref,
-    pressure_ref,
-    sat_ref,
-    perm_ref,
-    porosity_ref,
-    flags_ref,
-    inverse_ref,
-    seismic_ref,
     in_sem,
     out_sem,
     mob,
@@ -162,8 +173,11 @@
             bit *= 2
         return number
 
+    flipped_y = [flip(here[1], bits) for bits in range(n_gy)]
+    flipped_z = [flip(here[2], bits) for bits in range(n_gz)]
+
     def peer(order):
-        return (here[0], flip(here[1], order // n_gz), flip(here[2], order % n_gz))
+        return (here[0], flipped_y[order // n_gz], flipped_z[order % n_gz])
 
     def peer_place(order):
         other = peer(order)
@@ -203,6 +217,17 @@
                 (saturation_hbm, sat_ref),
                 (perm_hbm, perm_ref),
                 (pressure_hbm, pressure_ref),
+                (well_x_hbm, well_x_ref),
+                (well_y_hbm, well_y_ref),
+                (well_top_hbm, well_top_ref),
+                (well_len_hbm, well_len_ref),
+                (bhp_hbm, bhp_ref),
+                (obs_hbm, obs_ref),
+                (fault_cell_hbm, fault_cell_ref),
+                (fault_count_hbm, fault_count_ref),
+                (fault_trans_hbm, fault_trans_ref),
+                (fault_up_hbm, fault_up_ref),
+                (map_hbm, map_ref),
                 (flags_hbm, flags_ref),
                 (seismic_hbm, seismic_ref),
                 (inverse_hbm, inverse_ref),
@@ -260,6 +285,8 @@
         for order in range(peers):
             target[order : order + 1, :] = array[pl.ds(peer_place(order), 1), :]
 
+    for load in loads[:14]:
+        load.wait()
     faults_in_order(fault_cell_ref.at[0], f_cell)
     faults_in_order(fault_up_ref.at[0], f_up)
     slot_index = lax.broadcasted_iota(jnp.int32, (1, slots), 1)
@@ -271,32 +298,19 @@
     f_row = f_cell[...] // nz
     f_z = f_cell[...] - f_row * nz
 
-    def gather_half(ref, low, high):
+    def gather(refs, low=0, high=None):
+        high = peers if high is None else high
         row, at = f_row[low:high], f_z[low:high]
 
         def body(x, chosen):
             for y in range(ny):
-                taken = jnp.take_along_axis(
-                    jnp.broadcast_to(ref[x, y : y + 1, :], (high - low, nz)),
-                    at,
-                    axis=1,
-                    mode="promise_in_bounds",
-                )
-                chosen = jnp.where(row == x * ny + y, taken, chosen)
-            return chosen
-
-        return lax.fori_loop(0, nx, body, jnp.zeros((high - low, slots), f32), unroll=True)
-
-    def gather(refs):
-        def body(x, chosen):
-            for y in range(ny):
-                here_row = f_row == x * ny + y
+                here_row = row == x * ny + y
                 chosen = [
                     jnp.where(
                         here_row,
                         jnp.take_along_axis(
-                            jnp.broadcast_to(ref[x, y : y + 1, :], (peers, nz)),
-                            f_z,
+                            jnp.broadcast_to(ref[x, y : y + 1, :], (high - low, nz)),
+                            at,
                             axis=1,
                             mode="promise_in_bounds",
                         ),
@@ -306,16 +320,13 @@
                 ]
             return chosen
 
-        start = [jnp.zeros((peers, slots), f32) for _ in refs]
+        start = [jnp.zeros((high - low, slots), f32) for _ in refs]
         return lax.fori_loop(0, nx, body, start, unroll=True)
 
-    loads[0].wait()
     mobility = [phase_mobility(sat_ref[t + 1, 0], sat_ref[t + 1, 1]) for t in range(2)]
     for t in range(2):
         for k in range(3):
             mob[t, k] = mobility[t][k]
-    for load in loads[1:4]:
-        load.wait()
     perm = perm_ref[...]
 
     def bundle(part, fields):
@@ -367,7 +378,6 @@
                 for copy in copies:
                     copy(dim, side).wait_recv()
 
-    bundle(0, [perm] + mobility[1] + [flags_ref[...].astype(f32)])
 
     n_wells = well_top_ref.shape[2]
     eye = lax.broadcasted_iota(jnp.int32, (n_wells, n_wells), 0) == lax.broadcasted_iota(
@@ -434,6 +444,8 @@
         )
         copy.start()
         w_copies.append(copy)
+    loads[14].wait()
+    bundle(0, [perm_ref[...]] + [mob[1, k] for k in range(3)] + [flags_ref[...].astype(f32)])
     start_faces([functools.partial(bundle_copy, 0)])
 
     def order_far_first():
@@ -494,7 +506,7 @@
         )
         return (added[:rows] + added[rows:]).reshape(shape)
 
-    for load in loads[4:]:
+    for load in loads[15:]:
         load.wait()
     for copy in w_copies:
         copy.wait()
@@ -613,7 +625,7 @@
     def send_faults(parity, ref, lead, fixed):
         for low in range(peers - 8, -8, -8):
             part = slice(low, low + 8)
-            values = f_send[lead, part] * gather_half(ref, low, low + 8)
+            values = f_send[lead, part] * gather([ref], low, low + 8)[0]
             if fixed is not None:
                 values = values + f_send[fixed, part]
             c_s[parity, part] = values
@@ -633,6 +645,7 @@
     def scalar_round(parity, t, aside):
         send_faults(parity, delta, t, None)
         now = delta[...]
+        total_r[...] += now
         inner = send_faces(
             parity,
             [push[t, 0, dim] * now for dim in range(3)],
@@ -643,7 +656,6 @@
         inner = add_faces(parity, inner)
         inner = add_faults(parity, inner)
         delta[...] = inner
-        total_r[...] += inner
 
     def dot3(coefficients, values):
         return sum(coefficients(k) * values(k) for k in range(3))
@@ -662,10 +674,6 @@
     for k in range(3):
         const[k] = inverse_ref[1, 1, k] * src[1, 1] + inverse_ref[1, 2, k] * src[1, 2]
         lam[1, k] = const[k] + inverse_ref[1, 0, k] * src[1, 0]
-    values = gather([lam.at[1, k] for k in range(3)])
-    for k in range(3):
-        v_s[k] = values[k]
-
     def vector_copy(low, high, to):
         return remote(
             v_s.at[:, low:high],
@@ -675,8 +683,12 @@
             to,
         )
 
-    for order in order_far_first():
-        vector_copy(order, order + 1, peer(order)).start()
+    for low in range(peers - 8, -8, -8):
+        values = gather([lam.at[1, k] for k in range(3)], low, low + 8)
+        for k in range(3):
+            v_s[k, low : low + 8] = values[k]
+        for order in range(low + 7, max(low, 1) - 1, -1):
+            vector_copy(order, order + 1, peer(order)).start()
     wait_faces([functools.partial(bundle_copy, 0)])
     flags = flags_ref[...].astype(f32)
     face_coefficients(1, flags, lambda k: (0, 1 + k))
@@ -701,7 +713,6 @@
         inner = inner + scatter(arrived, low, high)
     vector_copy(1, peers, peer(1)).wait_send()
     delta[...] = inner
-    total_r[...] += inner
 
     def prepare_turn():
         explicit[...] += sources(0)
@@ -746,6 +757,7 @@
     out_late = pltpu.make_async_copy(lam.at[1], lam_hbm.at[1], out_sem.at[1])
     out_early = pltpu.make_async_copy(lam.at[0], lam_hbm.at[0], out_sem.at[0])
     parity = n_rounds % 2
+    total_r[...] += delta[...]
     send_faults(parity, total_r, 3, 2)
     now = total_r[...]
     inner = send_faces(
@@ -766,7 +778,7 @@
     inner = add_faces(parity, inner)
     inner = add_faults(parity, inner)
     delta[...] = inner
-    total_r[...] = src[0, 0] + inner
+    total_r[...] = src[0, 0]
 
     n_bx, n_by, n_bz = nx // BOX, ny // BOX, nz // BOX
     n_boxes = n_bx * n_by
@@ -860,6 +872,7 @@
     scalar_round(parity, 0, prepare_gradient)
     lax.fori_loop(n_rounds + 2, 2 * n_rounds, more(0), 0)
 
+    total_r[...] += delta[...]
     now = total_r[...]
     flux = [
         [flux_base[side, dim] + flux_lead[side, dim] * now for dim in range(3)]
@@ -1009,10 +1022,9 @@
 
     bundles = [(2, 2, 5, ny, nz), (2, 2, 5, nx, 1, nz), (2, 2, 5, ny, nz)]
     faces = [(2, ny, nz), (2, nx, 1, nz), (2, ny, nz)]
-    large = arrays[:7]
     scratch = [
-        *[pltpu.VMEM(array.shape, array.dtype) for array in large],
-        dma((len(large),)),
+        *[pltpu.VMEM(array.shape, array.dtype) for array in arrays],
+        dma((len(arrays),)),
         dma((2,)),
         field(2, 3),
         field(2, 3, 3),
@@ -1079,7 +1091,7 @@
     found = pl.pallas_call(
         functools.partial(kernel, counts),
         out_shape=results,
-        in_specs=[hbm] * 7 + [vmem] * 11,
+        in_specs=[hbm] * len(arrays),
         out_specs=(hbm, vmem),
         scratch_shapes=scratch,
         compiler_params=pltpu.CompilerParams(

time: 65.1 us -> 64.1 us (0.985)
  Pallas kernels: 64.1 us -> 63.1 us
    pallas_call x1, Pallas kernels: 61.8 us -> 60.8 us  [local(): pl.pallas_call(functools.partial(kernel, counts), out_shape=results, in_s...]
where the time goes in v4:
time: 64.1 us; the launch traced here: 63.9 us
  Pallas kernels  63.1 us (98%)
  between operations  0.81 us (1%)
    pallas_call x1, Pallas kernels, local(): pl.pallas_call(functools.partial(kernel, counts), out_shape=results, in_s...  60.8 us
    pallas_call x1, Pallas kernels, local(): pl.pallas_call(finish, out_shape=results, in_specs=[vmem, vmem], out_spec...  2.31 us

profile of v4, /device:TPU:0, one launch (start us, length us, event | category | flops | bytes accessed | tf_op | source)
XLA Modules:
  0.0 63.9 jit_solution(12012842487671696968)
XLA Ops:
  0.6 60.8 %shard_map.185 = (f32[2,3,16,8,128]{4,3,2,1,0:T(8,128)}, f32[2,32]{1,0:T(2,128)}) custom-call(f32[2,16,8,128]{3,2,1,0:T(8,128)} %pressure_hbm.1, f32[3,2,16,8,128]{4,3,2,1,0:T(8,128)} %saturation_hbm.1, f32[16,8,128]{2,1,0:T(8,128)} %perm_hbm.1, f32[16,8,128]{2,1,0:T(8,128)} %porosity_hbm.1, s32[16,8,128]{2,1,0:T(8,128)} %flags_hbm.1, ...), custom_call_target="tpu_custom_call" | custom-call | tf_op jit(solution)/shard_map/pallas_call | solution.py:1091
  61.5 2.3 %shard_map.186 = (f32[2,3,16,8,128]{4,3,2,1,0:T(8,128)}, f32[2,32]{1,0:T(2,128)}) custom-call(f32[2,3,16,8,128]{4,3,2,1,0:T(8,128)} %get-tuple-element.4.lam_ref, f32[2,32]{1,0:T(2,128)} %get-tuple-element.5.region_ref), custom_call_target="tpu_custom_call" | custom-call | tf_op jit(solution)/shard_map/pallas_call | solution.py:1108

commit v5 on v4

--- a/solution.py
+++ b/solution.py
@@ -516,14 +516,14 @@
 
     def sources(t):
         misfit = (rates[t : t + 1, :n_wells] - obs_ref[t, 0]) / sigma_sq
-        weighted = well_hot_t * misfit
-        both = jnp.concatenate([weighted, weighted * bhp_ref[t, 0]], axis=0)
+        weighted = perforated * as_column(misfit)
+        both = jnp.concatenate([weighted, weighted * as_column(bhp_ref[t, 0])], axis=1)
         spread = jnp.dot(
+            jnp.concatenate([well_hot_t.astype(jnp.bfloat16)] * 3, axis=1),
             jnp.concatenate(split(both, 3), axis=0),
-            perforated.astype(jnp.bfloat16),
             preferred_element_type=f32,
         )
-        spread = spread[: 2 * rows] + spread[2 * rows : 4 * rows] + spread[4 * rows :]
+        spread = jnp.concatenate([spread[:, :nz], spread[:, nz:]], axis=0)
         drawn = pressure_ref[t] * spread[:rows].reshape(shape) - spread[rows:].reshape(shape)
         water_slope, oil_slope = mobility_slopes(sat_ref[t + 1, 0], sat_ref[t + 1, 1])
         whole = total(t)

time: 64.1 us -> 64.1 us (level)
  no operation moved by 1% of the time
where the time goes in v5:
time: 64.1 us; the launch traced here: 63.9 us
  Pallas kernels  63.1 us (98%)
  between operations  0.81 us (1%)
    pallas_call x1, Pallas kernels, local(): pl.pallas_call(functools.partial(kernel, counts), out_shape=results, in_s...  60.8 us
    pallas_call x1, Pallas kernels, local(): pl.pallas_call(finish, out_shape=results, in_specs=[vmem, vmem], out_spec...  2.31 us

profile of v5, /device:TPU:0, one launch (start us, length us, event | category | flops | bytes accessed | tf_op | source)
XLA Modules:
  0.0 63.9 jit_solution(4313414470700942172)
XLA Ops:
  0.6 60.8 %shard_map.185 = (f32[2,3,16,8,128]{4,3,2,1,0:T(8,128)}, f32[2,32]{1,0:T(2,128)}) custom-call(f32[2,16,8,128]{3,2,1,0:T(8,128)} %pressure_hbm.1, f32[3,2,16,8,128]{4,3,2,1,0:T(8,128)} %saturation_hbm.1, f32[16,8,128]{2,1,0:T(8,128)} %perm_hbm.1, f32[16,8,128]{2,1,0:T(8,128)} %porosity_hbm.1, s32[16,8,128]{2,1,0:T(8,128)} %flags_hbm.1, ...), custom_call_target="tpu_custom_call" | custom-call | tf_op jit(solution)/shard_map/pallas_call | solution.py:1091
  61.4 2.3 %shard_map.186 = (f32[2,3,16,8,128]{4,3,2,1,0:T(8,128)}, f32[2,32]{1,0:T(2,128)}) custom-call(f32[2,3,16,8,128]{4,3,2,1,0:T(8,128)} %get-tuple-element.4.lam_ref, f32[2,32]{1,0:T(2,128)} %get-tuple-element.5.region_ref), custom_call_target="tpu_custom_call" | custom-call | tf_op jit(solution)/shard_map/pallas_call | solution.py:1108
